TPU v7x, 256 devices: a whole 4x4x8 slice. The times are simulated.
256 devices in a mesh: dp: 16 (over x_hi, y, core), tensor: 16 (over x_lo, z).
Axes of the slice: x: 4 (x_hi: 2, x_lo: 2; x = x_hi * 2 + x_lo), y: 4, z: 8, core: 2. Of those that a mesh axis runs over, the one named last changes fastest.
Arguments:
- tokens_in: bfloat16 [2048, 8192], P('dp'), may hold values from -6 to 6
- proj_gate: bfloat16 [8192, 8192], P('dp', 'tensor'), may hold values from -0.0625 to 0.0625
- proj_value: bfloat16 [8192, 8192], P('dp', 'tensor')
- state_in: bfloat16 [8192, 128], P('tensor'), may hold values from -0.0625 to 0.0625
- state_out: bfloat16 [8192, 128], P('tensor'), may hold values from -0.0625 to 0.0625
- proj_step: bfloat16 [8192, 128], P('tensor'), may hold values from -0.0625 to 0.0625
- step_bias: float32 [128], P('tensor'), may hold values from -4 to -1
- decay_log: float32 [128], P('tensor'), may hold values from -1 to 1.5
- skip_scale: float32 [128], P('tensor'), may hold values from 0.5 to 1.5
- norm_gain: float32 [8192], P('tensor'), may hold values from 0.5 to 1.5
- proj_output: bfloat16 [8192, 8192], P('dp', 'tensor'), may hold values from -0.0625 to 0.0625
- upstream: bfloat16 [2048, 8192], P('dp'), may hold values from -6 to 6
Outputs:
- layer_out: bfloat16 [2048, 8192], P('dp')
- input_grad: bfloat16 [2048, 8192], P('dp')
- grad_gate: float32 [8192, 8192], P('dp', 'tensor')
- grad_value: float32 [8192, 8192], P('dp', 'tensor')
- grad_output: float32 [8192, 8192], P('dp', 'tensor')
- grad_state_in: float32 [8192, 128], P('tensor')
- grad_state_out: float32 [8192, 128], P('tensor')
- grad_step: float32 [8192, 128], P('tensor')
- grad_bias: float32 [128], P('tensor')
- grad_decay: float32 [128], P('tensor')
- grad_skip: float32 [128], P('tensor')
- grad_gain: float32 [8192], P('tensor')
All inputs are finite; a program needn't handle non-finite values.
Results may differ from a plain program's by a relative error of at most 0.0051.
Values may be sent and summed in bfloat16 or wider, within the bound.
A program may use at most 192 MiB of HBM per device.

v0:
```python
import jax
import jax.numpy as jnp
from jax import lax
from jax.sharding import PartitionSpec as P

HEADS = 128
HDIM = 64


HIGH = lax.Precision.HIGHEST
EPS = 1e-05


def state_mix(gate_pre, value_pre, mat_b, mat_c, step_raw, step_bias, decay_log, skip_scale):
    length = value_pre.shape[0]
    heads = step_raw.shape[1]
    step_size = jax.nn.softplus(step_raw + step_bias)
    rate = jnp.exp(decay_log) * step_size
    cumulative = jnp.cumsum(rate, axis=0)
    affinity = jnp.dot(mat_c, mat_b.T, precision=HIGH)
    position = jnp.arange(length)
    causal = (position[:, None] >= position[None, :])[:, :, None]
    spread = cumulative[:, None, :] - cumulative[None, :, :]
    spread = jnp.where(causal, spread, jnp.float32(0.0))
    kernel = (
        jnp.where(causal, jnp.exp(-spread), jnp.float32(0.0))
        * affinity[:, :, None]
        * step_size[None, :, :]
    )
    per_head = value_pre.reshape(length, heads, -1)
    outputs = (
        jnp.einsum("tsh,shp->thp", kernel, per_head, precision=HIGH)
        + skip_scale[None, :, None] * per_head
    )
    return outputs.reshape(length, -1) * jax.nn.silu(gate_pre)


def contract_rows(left, right):
    return lax.dot_general(
        left, right, (((0,), (0,)), ((), ())), preferred_element_type=jnp.float32
    )


def contract_cols(left, right):
    return lax.dot_general(
        left, right, (((1,), (1,)), ((), ())), preferred_element_type=jnp.float32
    )


def per_device(
    tokens_in,
    proj_gate,
    proj_value,
    state_in,
    state_out,
    proj_step,
    step_bias,
    decay_log,
    skip_scale,
    norm_gain,
    proj_output,
    upstream,
):
    f32 = jnp.float32
    bf16 = jnp.bfloat16
    length = tokens_in.shape[0]
    slab = state_in.shape[0]
    local_width = proj_gate.shape[1]
    local_heads = step_bias.shape[0]
    all_heads = proj_step.shape[1]
    inner = HEADS * HDIM
    tensor_pos = lax.axis_index("tensor")
    feature_slab = lax.dynamic_slice_in_dim(tokens_in, tensor_pos * slab, slab, 1)
    mat_b, mat_c, step_all = lax.psum(
        (
            jnp.dot(feature_slab, state_in, preferred_element_type=f32),
            jnp.dot(feature_slab, state_out, preferred_element_type=f32),
            jnp.dot(feature_slab, proj_step, preferred_element_type=f32),
        ),
        "tensor",
    )
    step_raw = lax.dynamic_slice_in_dim(step_all, tensor_pos * local_heads, local_heads, 1)
    full_gate, full_value = (
        lax.all_gather(proj_gate, "dp", axis=0, tiled=True),
        lax.all_gather(proj_value, "dp", axis=0, tiled=True),
    )
    gate_pre = jnp.dot(tokens_in, full_gate, preferred_element_type=f32)
    value_pre = jnp.dot(tokens_in, full_value, preferred_element_type=f32)
    gated, pull = jax.vjp(
        state_mix, gate_pre, value_pre, mat_b, mat_c, step_raw, step_bias, decay_log, skip_scale
    )
    square_sum = lax.psum(jnp.sum(gated * gated, axis=1), "tensor")
    inv_rms = lax.rsqrt(square_sum / inner + EPS)
    normed = (gated * inv_rms[:, None] * norm_gain).astype(bf16)
    full_output = lax.all_gather(proj_output, "dp", axis=0, tiled=True)
    layer_part = contract_cols(normed, full_output)
    out_share = lax.psum_scatter(layer_part, "tensor", scatter_dimension=1, tiled=True)
    layer_out = lax.all_gather(out_share.astype(bf16), "tensor", axis=1, tiled=True)
    grad_normed = jnp.dot(upstream, full_output, preferred_element_type=f32)
    piece = upstream
    grad_output = lax.psum_scatter(
        contract_rows(piece, normed), "dp", scatter_dimension=0, tiled=True
    )
    scaled = grad_normed * norm_gain
    gain_local = jnp.sum(grad_normed * gated * inv_rms[:, None], axis=0)
    dot_total = lax.psum(jnp.sum(scaled * gated, axis=1), "tensor")
    grad_gated = inv_rms[:, None] * scaled - gated * (inv_rms**3 * dot_total / inner)[:, None]
    gate_back, value_back, back_b, back_c, step_back, bias_local, decay_local, skip_local = pull(
        grad_gated
    )
    step_padded = lax.dynamic_update_slice_in_dim(
        jnp.zeros((length, all_heads), f32), step_back, tensor_pos * local_heads, 1
    )
    sum_b, sum_c, sum_step = lax.psum((back_b, back_c, step_padded), "tensor")
    b_low = sum_b.astype(bf16)
    c_low = sum_c.astype(bf16)
    step_low = sum_step.astype(bf16)
    side_back = (
        contract_cols(b_low, state_in)
        + contract_cols(c_low, state_out)
        + contract_cols(step_low, proj_step)
    )
    grad_state_in, grad_state_out, grad_step, grad_bias, grad_decay, grad_skip, grad_gain = (
        lax.psum(
            (
                contract_rows(feature_slab, b_low),
                contract_rows(feature_slab, c_low),
                contract_rows(feature_slab, step_low),
                bias_local,
                decay_local,
                skip_local,
                gain_local,
            ),
            "dp",
        )
    )
    grad_both = jnp.concatenate([gate_back, value_back], axis=1).astype(bf16)
    piece = tokens_in
    both_grad = lax.psum_scatter(
        contract_rows(piece, grad_both), "dp", scatter_dimension=0, tiled=True
    )
    input_part = contract_cols(grad_both[:, :local_width], full_gate) + contract_cols(
        grad_both[:, local_width:], full_value
    )
    grad_gate = both_grad[:, :local_width]
    grad_value = both_grad[:, local_width:]
    dense = lax.psum(input_part, "tensor")
    side_all = lax.all_gather(side_back, "tensor", axis=1, tiled=True)
    input_grad = (dense + side_all).astype(bf16)
    return (
        layer_out,
        input_grad,
        grad_gate,
        grad_value,
        grad_output,
        grad_state_in,
        grad_state_out,
        grad_step,
        grad_bias,
        grad_decay,
        grad_skip,
        grad_gain,
    )


def solution(mesh):
    placed = (
        P("dp", None),
        P("dp", "tensor"),
        P("dp", "tensor"),
        P("tensor", None),
        P("tensor", None),
        P("tensor", None),
        P("tensor"),
        P("tensor"),
        P("tensor"),
        P("tensor"),
        P("dp", "tensor"),
        P("dp", None),
    )
    return jax.shard_map(
        per_device,
        mesh=mesh,
        in_specs=placed,
        out_specs=(
            P("dp", None),
            P("dp", None),
            P("dp", "tensor"),
            P("dp", "tensor"),
            P("dp", "tensor"),
            P("tensor", None),
            P("tensor", None),
            P("tensor", None),
            P("tensor"),
            P("tensor"),
            P("tensor"),
            P("tensor"),
        ),
        check_vma=False,
    )
```

profile of v0, /device:TPU:2, one launch (start us, length us, event | category | flops | bytes accessed | tf_op | source)
XLA Modules:
  0.0 907.7 jit_solution(15792819525304083753)
XLA Ops:
  17.3 131.5 %all-reduce.11.cloned.1.call-done = (f32[128,128]{0,1:T(8,128)}, f32[128,128]{1,0:T(8,128)}, f32[128,128]{1,0:T(8,128)}) async-done(((f32[128,128]{0,1:T(8,128)}, f32[128,128]{1,0:T(8,128)}, f32[128,128]{1,0:T(8,128)}), (f32[128,128]{0,1:T(8,128)}, f32[128,128]{1,0:T(8,128)}, f32[128,128]{1,0:T(8,128)})) %all-reduce.11.cloned.1.call-update) | async-done | bytes 196624 | tf_op jit(solution)/shard_map/psum | solution.py:74
  151.1 4.6 fusion.70
  157.3 19.9 %all-gather.8.cloned.1.call-done = bf16[8192,512]{1,0:T(8,128)(2,1)} async-done(((bf16[512,512]{1,0:T(8,128)(2,1)}), bf16[8192,512]{1,0:T(8,128)(2,1)}) %all-gather.8.cloned.1.call-update) | async-done | bytes 8388624 | tf_op jit(solution)/shard_map/all_gather | solution.py:84
  177.2 4.8 multiply_reduce_fusion.5
  182.0 34.8 %psum.115 = f32[128]{0:T(128)S(1)} all-reduce(f32[128]{0:T(128)S(1)} %get-tuple-element.83), channel_id=1, replica_groups=mesh['dp'=16,'tensor'=16] {'tensor'}, use_global_device_ids=true, to_apply=%region_5.6 | all-reduce | flops 128 | bytes 1024 | tf_op jit(solution)/shard_map/psum | solution.py:92
  216.8 38.7 %all-gather.10.cloned.1.call-done = bf16[8192,512]{1,0:T(8,128)(2,1)} async-done(((bf16[512,512]{1,0:T(8,128)(2,1)}), bf16[8192,512]{1,0:T(8,128)(2,1)}) %all-gather.10.cloned.1.call-update) | async-done | bytes 8388624 | tf_op jit(solution)/shard_map/all_gather | solution.py:95
  255.5 8.2 fusion.64
  263.8 6.0 multiply_reduce_fusion.2
  269.8 35.1 %psum.116 = f32[128]{0:T(128)S(1)} all-reduce(f32[128]{0:T(128)S(1)} %get-tuple-element.65), channel_id=1, replica_groups=mesh['dp'=16,'tensor'=16] {'tensor'}, use_global_device_ids=true, to_apply=%region_8.9 | all-reduce | flops 128 | bytes 1024 | tf_op jit(solution)/shard_map/psum | solution.py:106
  308.6 6.3 fusion.72
  314.9 8.4 convolution_add_fusion
  329.3 62.3 %all-reduce.14 = (bf16[128,128]{1,0:T(8,128)(2,1)S(1)}, bf16[128,128]{1,0:T(8,128)(2,1)S(1)}, bf16[128,128]{0,1:T(8,128)(2,1)S(1)}) all-reduce(f32[128,128]{1,0:T(8,128)S(1)} %fusion.73, f32[128,128]{1,0:T(8,128)S(1)} %fusion.74, f32[128,128]{0,1:T(8,128)S(1)} %constant_dynamic-update-slice_fusion), channel_id=1, replica_groups=mesh['dp'=16,'tensor'=16] {'tensor'}, use_global_device_ids=true, to_apply=%region_11.12 | all-reduce | flops 49152 | bytes 294912 | tf_op jit(solution)/shard_map/psum | solution.py:114
  394.7 9.7 %convolution_bitcast_fusion.1 = f32[8192,512]{0,1:T(8,128)} fusion(bf16[128,8192]{1,0:T(8,128)(2,1)} %param.23, f32[128,512]{1,0:T(8,128)S(1)} %get-tuple-element.84, f32[512]{0:T(512)S(1)} %copy-done.11, f32[128]{0:T(128)S(1)} %add_rsqrt_fusion), kind=kOutput, calls=%fused_computation.1 | convolution fusion | flops 1073938432 | bytes 19139072 | tf_op jit(solution)/shard_map/dot_general | solution.py:39
  404.9 19.3 %convolution_bitcast_fusion = f32[8192,1024]{0,1:T(8,128)} fusion(bf16[128,8192]{1,0:T(8,128)(2,1)S(1)} %copy-done, bf16[128,512]{1,0:T(8,128)(2,1)S(1)} %copy.75, bf16[128,512]{1,0:T(8,128)(2,1)S(1)} %get-tuple-element.89), kind=kOutput, calls=%fused_computation | convolution fusion | flops 2148007936 | bytes 35913728 | tf_op jit(solution)/shard_map/dot_general | solution.py:39
  427.6 37.5 %all-reduce.2 = (f32[8]{0:T(128)}, f32[8]{0:T(128)}, f32[8]{0:T(128)}, f32[512]{0:T(512)}) all-reduce(f32[8]{0:T(128)S(1)} %get-tuple-element.81, f32[8]{0:T(128)S(1)} %exponential_multiply_fusion, f32[8]{0:T(128)S(1)} %reduce_sum.118, f32[512]{0:T(512)S(1)} %copy-done.16), channel_id=1, replica_groups=mesh['dp'=16,'tensor'=16] {'dp'}, use_global_device_ids=true, to_apply=%region_24.25 | all-reduce | flops 536 | bytes 4288 | tf_op jit(solution)/shard_map/psum | solution.py:124
  465.1 30.0 %all-reduce.9.cloned.1.call-done = f32[128,8192]{1,0:T(8,128)} async-done(((f32[128,8192]{1,0:T(8,128)}), f32[128,8192]{1,0:T(8,128)}) %all-reduce.9.cloned.1.call-update) | async-done | bytes 4194320 | tf_op jit(solution)/shard_map/psum | solution.py:147
  495.1 77.7 %all-gather.14.cloned.1.call-done = f32[128,8192]{1,0:T(8,128)} async-done(((f32[128,512]{1,0:T(8,128)}), f32[128,8192]{1,0:T(8,128)}) %all-gather.14.cloned.1.call-update) | async-done | bytes 4194320 | tf_op jit(solution)/shard_map/all_gather | solution.py:148
  572.9 5.2 add_convert_fusion
  578.1 66.5 %all-gather.12.cloned.1.call-done = bf16[128,8192]{1,0:T(8,128)(2,1)} async-done(((bf16[128,512]{1,0:T(8,128)(2,1)}), bf16[128,8192]{1,0:T(8,128)(2,1)}) %all-gather.12.cloned.1.call-update) | async-done | bytes 2097168 | tf_op jit(solution)/shard_map/all_gather | solution.py:98
  644.6 2.7 copy.79
  647.3 241.0 %reduce-scatter.6.cloned.1.call-done = f32[512,1024]{0,1:T(8,128)} async-done(((f32[8192,1024]{0,1:T(8,128)}), f32[512,1024]{0,1:T(8,128)}) %reduce-scatter.6.cloned.1.call-update) | async-done | bytes 2097168 | tf_op jit(solution)/shard_map/reduce_scatter | solution.py:139
  888.3 2.7 fusion.69
  890.9 2.5 copy.77
  894.8 3.2 copy.95
  (117 shorter events, 32.9 us)
Async XLA Ops:
  8.0 140.8 %all-reduce.11.cloned.1.call-start = ((), (), s32[]{:S(2)}) async-start(), calls=%async_computation.12 | async-start | bytes 393216 | tf_op jit(solution)/shard_map/psum | solution.py:74
  14.8 136.3 %all-gather.6.cloned.1.call-start = ((), (), s32[]{:S(2)}) async-start(), calls=%async_computation.3 | async-start | bytes 8912896 | tf_op jit(solution)/shard_map/all_gather | solution.py:85
  15.4 161.8 %all-gather.8.cloned.1.call-start = ((), (), s32[]{:S(2)}) async-start(), calls=%async_computation.4 | async-start | bytes 8912896 | tf_op jit(solution)/shard_map/all_gather | solution.py:84
  16.0 239.6 %all-gather.10.cloned.1.call-start = ((), (), s32[]{:S(2)}) async-start(), calls=%async_computation.5 | async-start | bytes 8912896 | tf_op jit(solution)/shard_map/all_gather | solution.py:95
  16.6 376.4 %reduce-scatter.4.cloned.1.call-start = ((), (), s32[]{:S(2)}) async-start(), calls=%async_computation.6 | async-start | bytes 4456448 | tf_op jit(solution)/shard_map/reduce_scatter | solution.py:97
  17.3 132.3 %copy-start.20 = (f32[8]{0:T(128)}, f32[8]{0:T(128)S(1)}, u32[]{:S(2)}) copy-start(f32[8]{0:T(128)S(1)} %exp.18) | copy-start | bytes 100
  17.3 138.6 %copy-start.14 = (pred[128,128]{1,0:T(8,128)(4,1)}, pred[128,128]{1,0:T(8,128)(4,1)S(1)}, u32[]{:S(2)}) copy-start(pred[128,128]{1,0:T(8,128)(4,1)S(1)} %iota_compare_fusion) | copy-start | bytes 49156
  149.9 6.0 copy-start.17
  151.1 4.9 copy-start.12
  151.1 4.9 copy-start.22
  157.3 98.2 %copy-start.11 = (f32[512]{0:T(512)S(1)}, f32[512]{0:T(512)}, u32[]{:S(2)}) copy-start(f32[512]{0:T(512)} %param.21) | copy-start | bytes 6148
  263.7 231.4 %all-reduce.9.cloned.1.call-start = ((), (), s32[]{:S(2)}) async-start(), calls=%async_computation.8 | async-start | bytes 8388608 | tf_op jit(solution)/shard_map/psum | solution.py:147
  306.8 8.0 copy-start.10
  323.3 5.0 copy-start.19
  323.3 5.0 copy-start.21
  323.3 68.2 %copy-start.1 = (bf16[512,128]{1,0:T(8,128)(2,1)S(1)}, bf16[512,128]{1,0:T(8,128)(2,1)}, u32[]{:S(2)}) copy-start(bf16[512,128]{1,0:T(8,128)(2,1)} %param.15) | copy-start | bytes 393220
  323.3 68.4 %copy-start.2 = (bf16[512,128]{1,0:T(8,128)(2,1)S(1)}, bf16[512,128]{1,0:T(8,128)(2,1)}, u32[]{:S(2)}) copy-start(bf16[512,128]{1,0:T(8,128)(2,1)} %param.16) | copy-start | bytes 393220
  323.4 68.6 %copy-start.3 = (bf16[512,128]{1,0:T(8,128)(2,1)S(1)}, bf16[512,128]{1,0:T(8,128)(2,1)}, u32[]{:S(2)}) copy-start(bf16[512,128]{1,0:T(8,128)(2,1)} %param.17) | copy-start | bytes 393220
  323.4 249.5 %all-gather.14.cloned.1.call-start = ((), (), s32[]{:S(2)}) async-start(), calls=%async_computation.9 | async-start | bytes 4456448 | tf_op jit(solution)/shard_map/all_gather | solution.py:148
  392.9 251.7 %all-gather.12.cloned.1.call-start = ((), (), s32[]{:S(2)}) async-start(), calls=%async_computation.7 | async-start | bytes 2228224 | tf_op jit(solution)/shard_map/all_gather | solution.py:98
  394.6 250.0 %reduce-scatter.8.cloned.1.call-start = ((), (), s32[]{:S(2)}) async-start(), calls=%async_computation.11 | async-start | bytes 17825792 | tf_op jit(solution)/shard_map/reduce_scatter | solution.py:101
  404.5 483.8 %reduce-scatter.6.cloned.1.call-start = ((), (), s32[]{:S(2)}) async-start(), calls=%async_computation.10 | async-start | bytes 35651584 | tf_op jit(solution)/shard_map/reduce_scatter | solution.py:139
  424.2 470.6 %all-reduce.13.cloned.1.call-start = ((), (), s32[]{:S(2)}) async-start(), calls=%async_computation.13 | async-start | bytes 1572864 | tf_op jit(solution)/shard_map/psum | solution.py:124
  894.8 4.6 copy-start.7
  (11 other events, 23.4 us)
Sparse Core Ops, SparseCore 0:
  14.9 133.8 all-reduce.10
  263.9 78.9 reduce-scatter.3
  345.7 149.3 all-reduce.8
  497.5 75.3 all-gather.13
  575.2 69.3 all-gather.11
  648.1 173.5 all-reduce.12
Sparse Core Ops, SparseCore 1:
  18.4 80.7 all-gather.5
  102.2 75.0 all-gather.7
  180.2 75.2 all-gather.9
  404.5 223.5 reduce-scatter.7
  633.6 254.6 reduce-scatter.5
where the time goes:
time: 909 us; the launch traced here: 908 us
  waiting for transfers between devices  607 us (67%)
  blocking collectives  170 us (19%)
  matrix products  83.4 us (9%)
  local copies, waits for them, and re-layouts  19.7 us (2%)
  between operations  16.2 us (2%)
  other arithmetic  10.9 us (1%)
    reduce_scatter x1, waiting for transfers between devices, per_device(): lax.psum_scatter(contract_rows(piece, grad_both), 'dp', scatter_dimension...  241 us
    psum x1, waiting for transfers between devices, per_device(): lax.psum((jnp.dot(feature_slab, state_in, preferred_element_type=f32), jn...  132 us
    all_gather x1, waiting for transfers between devices, per_device(): side_all = lax.all_gather(side_back, 'tensor', axis=1, tiled=True)  77.7 us
    all_gather x1, waiting for transfers between devices, per_device(): lax.all_gather(out_share.astype(bf16), 'tensor', axis=1, tiled=True)  66.5 us
    psum x1, blocking collectives, per_device(): sum_b, sum_c, sum_step = lax.psum((back_b, back_c, step_padded), 'tensor')  62.3 us
    all_gather x1, waiting for transfers between devices, per_device(): full_output = lax.all_gather(proj_output, 'dp', axis=0, tiled=True)  38.7 us
    psum x1, blocking collectives, per_device(): lax.psum((contract_rows(feature_slab, b_low), contract_rows(feature_slab,...  37.5 us
    psum x1, blocking collectives, per_device(): dot_total = lax.psum(jnp.sum(scaled * gated, axis=1), 'tensor')  35.1 us
  transfers between devices with their start and end apart: 11, of which 7 were waited for; matrix products, arithmetic and copies ran while one was open for 10% of the time, Pallas kernels for 0%

commit v1 on v0

v1 whole, which is shorter than its diff:
```python
import jax
import jax.numpy as jnp
from jax import lax
from jax.experimental import pallas as pl
from jax.experimental.pallas import tpu as pltpu
from jax.sharding import PartitionSpec as P

MESH = pl.DeviceIdType.MESH
HIGH = lax.Precision.HIGHEST
EPS = 1e-05
INNER = 8192
F32 = jnp.float32
BF16 = jnp.bfloat16
VMEM_LIMIT = 58 * 2**20


def coords():
    d = lax.axis_index("dp")
    t = lax.axis_index("tensor")
    return d // 8, (d // 2) % 4, d % 2, t // 8, t % 8


def place(x_hi, y, core, x_lo, z):
    return (x_hi * 8 + y * 2 + core, x_lo * 8 + z)


def announce(devices):
    barrier = pltpu.get_barrier_semaphore()
    for device in devices:
        pl.semaphore_signal(barrier, inc=1, device_id=device, device_id_type=MESH)


def gathered(count):
    pl.semaphore_wait(pltpu.get_barrier_semaphore(), count)


def chip_peer(j):
    x_hi, y, core, x_lo, z = coords()
    return place((x_hi + j // 4) % 2, (y + j % 4) % 4, core, x_lo, z)


def core_peer():
    x_hi, y, core, x_lo, z = coords()
    return place(x_hi, y, 1 - core, x_lo, z)


def tensor_peer(j):
    x_hi, y, core, x_lo, z = coords()
    return place(x_hi, y, core, (x_lo + j // 8) % 2, (z + j % 8) % 8)


def tensor_place(j):
    x_hi, y, core, x_lo, z = coords()
    return ((x_lo + j // 8) % 2) * 8 + (z + j % 8) % 8


def drive(steps, count=1):
    for _ in range(count):
        next(steps, None)


def finish(steps):
    for _ in steps:
        pass


def remote(src, dst, send, recv, device):
    return pltpu.make_async_remote_copy(
        src_ref=src, dst_ref=dst, send_sem=send, recv_sem=recv, device_id=device, device_id_type=MESH
    )


def dot(a, b):
    return jnp.dot(a, b, preferred_element_type=F32)


def dot_rows(a, b):
    return lax.dot_general(a, b, (((0,), (0,)), ((), ())), preferred_element_type=F32)


def dot_cols(a, b):
    return lax.dot_general(a, b, (((1,), (1,)), ((), ())), preferred_element_type=F32)


def halves(a):
    high = a.astype(BF16)
    return high, (a - high.astype(F32)).astype(BF16)


def three(product, a, b):
    a_high, a_low = halves(a)
    b_high, b_low = halves(b)
    return product(a_high, b_high) + (product(a_high, b_low) + product(a_low, b_high))


def vmem():
    return pl.BlockSpec(memory_space=pltpu.VMEM)


def params(cid):
    return pltpu.CompilerParams(collective_id=cid, has_side_effects=True, vmem_limit_bytes=VMEM_LIMIT)


def total_steps(part, slots, sum_ref, full, send, recv, again_send, again_recv):
    me = tensor_place(0)

    def scatter(j):
        return remote(part.at[tensor_place(j)], slots.at[me], send.at[j], recv.at[j], tensor_peer(j))

    def gather(j):
        return remote(sum_ref, full.at[me], again_send.at[j], again_recv.at[j], tensor_peer(j))

    for j in range(1, 16):
        scatter(j).start()
    slots[me] = part[me]
    yield
    for j in range(1, 16):
        scatter(j).wait()
    result = slots[0]
    for i in range(1, 16):
        result = result + slots[i]
    sum_ref[...] = result
    for j in range(1, 16):
        gather(j).start()
    full[me] = result
    yield
    for j in range(1, 16):
        gather(j).wait()


def total_scratch():
    sem = pltpu.SemaphoreType.DMA
    return [
        pltpu.VMEM((16, 8, 384), F32),
        pltpu.VMEM((16, 8, 384), F32),
        pltpu.VMEM((8, 384), F32),
        sem((16,)), sem((16,)), sem((16,)), sem((16,)),
    ]


def gather_steps(block, a_send, a_recv, b_send, b_recv):
    x_hi, y, core, x_lo, z = coords()
    up = place(x_hi, y, core, x_lo, (z + 1) % 8)
    down = place(x_hi, y, core, x_lo, (z + 7) % 8)
    across = place(x_hi, y, core, 1 - x_lo, z)
    own = block(x_lo, z)
    cross = remote(own, own, a_send, a_recv, across)
    cross.start()

    def copy(way, step, other):
        level = (z + 8 - step) % 8 if way == 0 else (z + step) % 8
        ref = block(1 - x_lo if other else x_lo, level)
        return remote(
            ref, ref, b_send.at[way, step, other], b_recv.at[way, step, other], up if way == 0 else down
        )

    def goes(way, step, other):
        return step < 3 or other == way

    for step in range(4):
        for other in (0, 1):
            if step == 0 and other == 1:
                cross.wait_recv()
            for way in (0, 1):
                if step > 0:
                    copy(way, step - 1, other).wait_recv()
                if goes(way, step, other):
                    copy(way, step, other).start()
        yield
    copy(0, 3, 0).wait_recv()
    copy(1, 3, 1).wait_recv()
    cross.wait_send()
    for step in range(4):
        for other in (0, 1):
            for way in (0, 1):
                if goes(way, step, other):
                    copy(way, step, other).wait_send()


def gather_scratch():
    sem = pltpu.SemaphoreType.DMA
    return [sem, sem, sem((2, 4, 2)), sem((2, 4, 2))]


def turn_peers():
    x_hi, y, core, x_lo, z = coords()
    turned = place(x_lo, (y + 4 - z // 2) % 4, core, x_hi, y * 2 + z % 2)
    turner = place(x_lo, z // 2, core, x_hi, ((z // 2 + 4 - y) % 4) * 2 + z % 2)
    stays = jnp.logical_and(x_lo == x_hi, jnp.logical_and(z // 2 == 0, y == 0))
    return turned, turner, stays


def reduce_steps(part, outbox, inbox, send, recv, xbox, xin, x_send, x_recv, tbox, tin, t_send, t_recv):
    x_hi, y, core, x_lo, z = coords()
    up = place(x_hi, y, core, x_lo, (z + 1) % 8)
    down = place(x_hi, y, core, x_lo, (z + 7) % 8)
    across = place(x_hi, y, core, 1 - x_lo, z)
    turned, turner, stays = turn_peers()

    def copy(way, step, block):
        return remote(
            outbox.at[way, step, block], inbox.at[way, step, block],
            send.at[way, step, block], recv.at[way, step, block], up if way == 0 else down,
        )

    def goes(way, step, block):
        return step > 0 or block == way

    for step in range(4):
        for block in (0, 1):
            for way in (0, 1):
                if not goes(way, step, block):
                    continue
                target = (z + 4 - step) % 8 if way == 0 else (z + 4 + step) % 8
                value = part[target, block]
                if step > 0 and goes(way, step - 1, block):
                    copy(way, step - 1, block).wait_recv()
                    value = value + inbox[way, step - 1, block].astype(F32)
                outbox[way, step, block] = value.astype(BF16)
                copy(way, step, block).start()
        yield
    for block in (0, 1):
        for way in (0, 1):
            copy(way, 3, block).wait_recv()
        part[z, block] = part[z, block] + (inbox[0, 3, block].astype(F32) + inbox[1, 3, block].astype(F32))
    xbox[...] = part[z, 1 - x_lo].astype(BF16)
    cross = remote(xbox, xin, x_send, x_recv, across)
    cross.start()
    yield
    for step in range(4):
        for block in (0, 1):
            for way in (0, 1):
                if goes(way, step, block):
                    copy(way, step, block).wait_send()
    cross.wait()
    tbox[...] = (part[z, x_lo] + xin[...].astype(F32)).astype(tbox.dtype)
    turn = remote(tbox, tin, t_send, t_recv, turned)

    @pl.when(stays)
    def _():
        tin[...] = tbox[...]

    @pl.when(jnp.logical_not(stays))
    def _():
        turn.start()

    yield

    @pl.when(jnp.logical_not(stays))
    def _():
        turn.wait()


def reduce_scratch(kind):
    sem = pltpu.SemaphoreType.DMA
    return [
        pltpu.VMEM((2, 4, 2, 128, 512), BF16),
        pltpu.VMEM((2, 4, 2, 128, 512), BF16),
        sem((2, 4, 2)), sem((2, 4, 2)),
        pltpu.VMEM((128, 512), BF16),
        pltpu.VMEM((128, 512), BF16),
        sem, sem,
        pltpu.VMEM((128, 512), kind),
        pltpu.VMEM((128, 512), kind),
        sem, sem,
    ]


def rows_first(part, result, inbox, send, recv, xin, x_send, x_recv):
    x_hi, y, core, x_lo, z = coords()
    ways = (place(x_hi, (y + 1) % 4, core, x_lo, z), place(x_hi, (y + 3) % 4, core, x_lo, z))
    across = place(1 - x_hi, y, core, x_lo, z)

    def copy(way, step, block):
        level = (y + 2) % 4 if step == 0 else (y + 1 + 2 * way) % 4
        return remote(
            part.at[block * 4 + level], inbox.at[way, step, block],
            send.at[way, step, block], recv.at[way, step, block], ways[way],
        )

    for way in (0, 1):
        copy(way, 0, way).start()
    for way in (0, 1):
        copy(way, 1, 1 - way).start()
    yield
    for way in (0, 1):
        copy(way, 0, way).wait_recv()
        level = (y + 1 + 2 * way) % 4
        part[way * 4 + level] = part[way * 4 + level] + inbox[way, 0, way]
        copy(way, 1, way).start()
    yield
    cross = remote(part.at[(1 - x_hi) * 4 + y], xin, x_send, x_recv, across)
    for block in (0, 1):
        for way in (0, 1):
            copy(way, 1, block).wait_recv()
        part[block * 4 + y] = part[block * 4 + y] + (inbox[0, 1, block] + inbox[1, 1, block])
    cross.start()
    yield
    cross.wait()
    result[...] = part[x_hi * 4 + y] + xin[...]
    for way in (0, 1):
        copy(way, 0, way).wait_send()
        for block in (0, 1):
            copy(way, 1, block).wait_send()


def rows_scratch():
    sem = pltpu.SemaphoreType.DMA
    return [
        pltpu.VMEM((2, 2, 2, 128, 512), F32),
        sem((2, 2, 2)), sem((2, 2, 2)),
        pltpu.VMEM((128, 512), F32),
        sem, sem,
    ]


def across_first(part, result, xin, x_send, x_recv, inbox, send, recv):
    x_hi, y, core, x_lo, z = coords()
    ways = (place(x_hi, (y + 1) % 4, core, x_lo, z), place(x_hi, (y + 3) % 4, core, x_lo, z))
    across = place(1 - x_hi, y, core, x_lo, z)
    far = (y + 2) % 4

    def cross(i):
        return remote(
            part.at[(1 - x_hi) * 4 + (y + i) % 4], xin.at[i], x_send.at[i], x_recv.at[i], across
        )

    def half(way):
        rows = pl.ds(64 * way, 64)
        return remote(
            part.at[x_hi * 4 + far, rows], inbox.at[way, 0, rows], send.at[way, 0], recv.at[way, 0], ways[way]
        )

    def whole(way):
        level = (y + 1 + 2 * way) % 4
        return remote(
            part.at[x_hi * 4 + level], inbox.at[way, 1], send.at[way, 1], recv.at[way, 1], ways[way]
        )

    def add(i):
        cross(i).wait_recv()
        at = x_hi * 4 + (y + i) % 4
        part[at] = part[at] + xin[i]

    for i in (2, 1, 3, 0):
        cross(i).start()
    yield
    add(2)
    for way in (0, 1):
        half(way).start()
    yield
    for way in (0, 1):
        add(1 + 2 * way)
        half(way).wait_recv()
        at = x_hi * 4 + (y + 1 + 2 * way) % 4
        rows = slice(64 * way, 64 * way + 64)
        part[at, rows, :] = part[at, rows, :] + inbox[way, 0, rows, :]
        whole(way).start()
    yield
    add(0)
    for way in (0, 1):
        whole(way).wait_recv()
    result[...] = part[x_hi * 4 + y] + (inbox[0, 1] + inbox[1, 1])
    for i in range(4):
        cross(i).wait_send()
    for way in (0, 1):
        half(way).wait_send()
        whole(way).wait_send()


def across_scratch():
    sem = pltpu.SemaphoreType.DMA
    return [
        pltpu.VMEM((4, 128, 512), F32),
        sem((4,)), sem((4,)),
        pltpu.VMEM((2, 2, 128, 512), F32),
        sem((2, 2)), sem((2, 2)),
    ]


def project_kernel(
    tok, up, wg, wv, wo, s_in, s_out, s_step,
    tokc, upc, wcat, wof, gate, value, gn, state,
    part_g, part_v, part_n, w_send, w_recv, t_send, t_recv, u_send, u_recv, *scratch,
):
    x_hi, y, core, x_lo, z = coords()
    chip = x_hi * 4 + y
    for_state, scratch = scratch[:7], scratch[7:]
    for_upstream, scratch = scratch[:4], scratch[4:]
    for_gate, scratch = scratch[:6], scratch[6:]
    for_value, for_normed = scratch[:6], scratch[6:]

    def to_chip(j):
        return ((x_hi + j // 4) % 2) * 4 + (y + j % 4) % 4

    def from_chip(j):
        return ((x_hi + j // 4) % 2) * 4 + (y + 4 - j % 4) % 4

    partner = core_peer()
    devices = [chip_peer(j) for j in range(1, 8)] + [partner] + [tensor_peer(j) for j in range(1, 16)]
    announce(devices)
    slab = tok[:, pl.ds(pl.multiple_of((x_lo * 8 + z) * 512, 512), 512)]
    state_part = for_state[0]
    for i, weights in enumerate((s_in, s_out, s_step)):
        state_part[:, :, 128 * i : 128 * i + 128] = dot(slab, weights[...]).reshape(16, 8, 128)
    gathered(len(devices))

    mine = pl.ds(pl.multiple_of(core * 512, 512), 512)
    w_copies = []
    for i, (src, dst) in enumerate(
        ((wg, wcat.at[mine, pl.ds(0, 512)]), (wv, wcat.at[mine, pl.ds(512, 512)]), (wo, wof.at[mine, :]))
    ):
        copy = remote(src, dst, w_send.at[i], w_recv.at[i], partner)
        copy.start()
        w_copies.append(copy)

    rows = pl.ds(pl.multiple_of(z * 16, 16), 16)
    side = pl.ds(pl.multiple_of(x_lo * 512, 512), 512)

    def up_copy(j):
        columns = pl.ds(pl.multiple_of(to_chip(j) * 1024 + x_lo * 512, 512), 512)
        return remote(up.at[rows, columns], upc.at[chip, rows, side], u_send.at[j], u_recv.at[j], chip_peer(j))

    def tok_copy(j):
        columns = pl.ds(pl.multiple_of(to_chip(j) * 1024, 1024), 1024)
        return remote(tok.at[:, columns], tokc.at[chip], t_send.at[j], t_recv.at[j], chip_peer(j))

    for j in range(1, 8):
        up_copy(j).start()
    state_steps = total_steps(state_part, for_state[1], for_state[2], state, *for_state[3:])
    drive(state_steps)
    for j in range(1, 8):
        tok_copy(j).start()

    wcat[mine, pl.ds(0, 512)] = wg[...]
    wcat[mine, pl.ds(512, 512)] = wv[...]
    wof[mine, :] = wo[...]
    tokc[chip] = tok[:, pl.ds(pl.multiple_of(chip * 1024, 1024), 1024)]
    upc[chip, rows, side] = up[rows, pl.ds(pl.multiple_of(chip * 1024 + x_lo * 512, 512), 512)]
    for j in range(1, 8):
        up_copy(j).wait()

    def up_block(at_side, level):
        return upc.at[
            :, pl.ds(pl.multiple_of(level * 16, 16), 16), pl.ds(pl.multiple_of(at_side * 512, 512), 512)
        ]

    up_steps = gather_steps(up_block, *for_upstream)
    drive(up_steps)
    drive(state_steps)
    for copy in w_copies:
        copy.wait()
    drive(up_steps, 2)

    def multiply(src):
        part_g[src] = dot(tokc[src], wcat[:, 0:512])
        part_v[src] = dot(tokc[src], wcat[:, 512:1024])

    multiply(chip)

    def serve(j, carry):
        tok_copy(j).wait()
        multiply(from_chip(j))
        return carry

    lax.fori_loop(1, 8, serve, 0)
    gate_steps = across_first(part_g, gate, *for_gate)
    value_steps = rows_first(part_v, value, *for_value)
    drive(value_steps)
    drive(gate_steps)
    finish(up_steps)

    def serve_upstream(src, carry):
        part_n[src] = dot(upc[src], wof[...])
        return carry

    lax.fori_loop(0, 8, serve_upstream, 0)
    normed_steps = rows_first(part_n, gn, *for_normed)
    drive(value_steps)
    drive(normed_steps)
    drive(gate_steps)
    finish(state_steps)
    drive(value_steps)
    drive(normed_steps)
    drive(gate_steps)
    drive(normed_steps)
    finish(value_steps)
    finish(gate_steps)
    finish(normed_steps)


def project(*args):
    sem = pltpu.SemaphoreType.DMA
    return pl.pallas_call(
        project_kernel,
        out_shape=(
            jax.ShapeDtypeStruct((8, 128, 1024), BF16),
            jax.ShapeDtypeStruct((8, 128, 1024), BF16),
            jax.ShapeDtypeStruct((1024, 1024), BF16),
            jax.ShapeDtypeStruct((1024, 512), BF16),
            jax.ShapeDtypeStruct((128, 512), F32),
            jax.ShapeDtypeStruct((128, 512), F32),
            jax.ShapeDtypeStruct((128, 512), F32),
            jax.ShapeDtypeStruct((16, 8, 384), F32),
        ),
        in_specs=[vmem()] * 8,
        out_specs=(vmem(),) * 8,
        scratch_shapes=[
            pltpu.VMEM((8, 128, 512), F32),
            pltpu.VMEM((8, 128, 512), F32),
            pltpu.VMEM((8, 128, 512), F32),
            sem((3,)), sem((3,)),
        ] + [sem((8,))] * 4 + total_scratch() + gather_scratch() + across_scratch() + rows_scratch() * 2,
        compiler_params=params(0),
        cost_estimate=pl.CostEstimate(flops=3 * 10**9, bytes_accessed=200 * 10**6, transcendentals=0),
        name="project",
    )(*args)


def columns_of(rows):
    pad = jnp.zeros((128 - rows.shape[0], 128), F32)
    return jnp.concatenate([rows, pad], axis=0).T


def decay_terms(raw, log, b, c):
    step = jnp.maximum(raw, 0.0) + jnp.log1p(jnp.exp(-jnp.abs(raw)))
    growth = jnp.exp(log)
    rate = growth * step
    first = lax.broadcasted_iota(jnp.int32, (128, 128), 0)
    second = lax.broadcasted_iota(jnp.int32, (128, 128), 1)
    upper = (first <= second).astype(F32)
    cumulative = jnp.dot(rate, upper, precision=HIGH, preferred_element_type=F32)
    affinity = lax.dot_general(c, b, (((1,), (1,)), ((), ())), precision=HIGH, preferred_element_type=F32)
    return raw, step, growth, rate, cumulative, affinity, first >= second


def decay_of(cumulative, cum_cols, causal, h):
    spread = jnp.where(causal, cum_cols[:, h : h + 1] - cumulative[h : h + 1, :], 0.0)
    return jnp.where(causal, jnp.exp(-spread), 0.0)


def split_pair(pair):
    lane = lax.broadcasted_iota(jnp.int32, pair.shape, 1)
    return jnp.concatenate([jnp.where(lane < 64, pair, 0.0), jnp.where(lane < 64, 0.0, pair)], axis=0)


def mix_kernel(
    gate, value, gn, state, heads, gain,
    normed, gate_low, value_low, backs, small,
    step_rows, mixed, gated, d_mixed, part, slots, send, recv,
):
    devices = [tensor_peer(j) for j in range(1, 16)]
    announce(devices)
    me = tensor_place(0)
    b = state[:, :, 0:128].reshape(128, 128)
    c = state[:, :, 128:256].reshape(128, 128)
    step_rows[...] = state[:, :, 256:384].reshape(128, 128).T
    own_heads = pl.ds(pl.multiple_of(me * 8, 8), 8)
    raw, step, growth, rate, cumulative, affinity, causal = decay_terms(
        step_rows[own_heads, :] + heads[:, 0:1], heads[:, 1:2], b, c
    )
    cum_cols = columns_of(cumulative)
    lane = lax.broadcasted_iota(jnp.int32, (128, 128), 1)
    decays = []
    for h in range(8):
        decays.append(decay_of(cumulative, cum_cols, causal, h))
    for p in range(4):
        lanes = slice(128 * p, 128 * p + 128)
        kernels = [decays[h] * affinity * step[h : h + 1, :] for h in (2 * p, 2 * p + 1)]
        pair = value[:, lanes]
        skip = jnp.where(lane < 64, heads[2 * p : 2 * p + 1, 2:3], heads[2 * p + 1 : 2 * p + 2, 2:3])
        mixed[:, lanes] = three(dot, jnp.concatenate(kernels, axis=1), split_pair(pair)) + skip * pair
    g = gate[...]
    sig = 1.0 / (1.0 + jnp.exp(-g))
    gated[...] = mixed[...] * (g * sig)
    square = jnp.sum(gated[...] * gated[...], axis=1, keepdims=True)
    inner = jnp.sum(gn[...] * gain[...] * gated[...], axis=1, keepdims=True)
    part[...] = jnp.where(lane == 0, square, jnp.where(lane == 1, inner, 0.0)).T[0:8, :]
    gathered(len(devices))

    def copy(j):
        return remote(part, slots.at[me], send.at[j], recv.at[j], tensor_peer(j))

    for j in range(1, 16):
        copy(j).start()
    slots[me] = part[...]
    for j in range(1, 16):
        copy(j).wait()
    sums = slots[0]
    for i in range(1, 16):
        sums = sums + slots[i]

    inv_row = lax.rsqrt(sums[0:1, :] * (1.0 / INNER) + EPS)
    pull_row = inv_row * inv_row * inv_row * sums[1:2, :] * (1.0 / INNER)
    token_cols = columns_of(jnp.concatenate([inv_row, pull_row, jnp.zeros((6, 128), F32)], axis=0))
    inv = token_cols[:, 0:1]
    pull = token_cols[:, 1:2]
    unit = gated[...] * inv
    normed[...] = (unit * gain[...]).astype(BF16)
    gain_sum = jnp.sum(gn[...] * unit, axis=0, keepdims=True)
    grad = inv * (gn[...] * gain[...]) - gated[...] * pull
    g = gate[...]
    sig = 1.0 / (1.0 + jnp.exp(-g))
    gate_low[...] = (grad * mixed[...] * (sig * (1.0 + g * (1.0 - sig)))).astype(BF16)
    d_mixed[...] = grad * (g * sig)
    skip_sum = jnp.sum(d_mixed[...] * value[...], axis=0, keepdims=True)
    d_affinity = jnp.zeros((128, 128), F32)
    row_sums = jnp.zeros((128, 128), F32)
    col_sums = []
    for p in range(4):
        lanes = slice(128 * p, 128 * p + 128)
        dm_pair = d_mixed[:, lanes]
        dm_split = split_pair(dm_pair)
        pair = value[:, lanes]
        d_kernel = three(dot_cols, dm_split, pair)
        kernels = []
        for i, h in enumerate((2 * p, 2 * p + 1)):
            decay = decays[h]
            step_h = step[h : h + 1, :]
            weighted = decay * d_kernel[128 * i : 128 * i + 128, :]
            d_affinity = d_affinity + weighted * step_h
            direct = weighted * affinity
            col_sums.append(jnp.sum(direct, axis=0, keepdims=True))
            row_sums = jnp.where(lane == h, jnp.sum(direct * step_h, axis=1, keepdims=True), row_sums)
            kernels.append(decay * affinity * step_h)
        skip = jnp.where(lane < 64, heads[2 * p : 2 * p + 1, 2:3], heads[2 * p + 1 : 2 * p + 2, 2:3])
        value_low[:, lanes] = (
            three(dot_rows, jnp.concatenate(kernels, axis=0), dm_split) + skip * dm_pair
        ).astype(BF16)
    direct_step = jnp.concatenate(col_sums, axis=0)
    d_cumulative = direct_step * step - row_sums.T[0:8, :]
    d_rate = jnp.dot(d_cumulative, causal.astype(F32), precision=HIGH, preferred_element_type=F32)
    d_raw = (direct_step + growth * d_rate) * (1.0 / (1.0 + jnp.exp(-raw)))
    step_rows[...] = jnp.zeros((128, 128), F32)
    step_rows[own_heads, :] = d_raw
    backs[:, 0:128] = three(dot_rows, d_affinity, c)
    backs[:, 128:256] = three(dot, d_affinity, b)
    backs[:, 256:384] = step_rows[...].T
    lane8 = lax.broadcasted_iota(jnp.int32, (8, 128), 1)
    bias_sum = jnp.sum(d_raw, axis=1, keepdims=True)
    decay_sum = jnp.sum(d_rate * rate, axis=1, keepdims=True)
    small[...] = jnp.zeros((16, 384), F32)
    small[0:1, :] = gain_sum[:, 0:384]
    small[1:2, 0:128] = gain_sum[:, 384:512]
    small[2:3, :] = skip_sum[:, 0:384]
    small[3:4, 0:128] = skip_sum[:, 384:512]
    small[8:16, 0:128] = jnp.where(lane8 == 0, bias_sum, jnp.where(lane8 == 1, decay_sum, 0.0))


def mix(*args):
    sem = pltpu.SemaphoreType.DMA
    return pl.pallas_call(
        mix_kernel,
        out_shape=(
            jax.ShapeDtypeStruct((128, 512), BF16),
            jax.ShapeDtypeStruct((128, 512), BF16),
            jax.ShapeDtypeStruct((128, 512), BF16),
            jax.ShapeDtypeStruct((128, 384), F32),
            jax.ShapeDtypeStruct((16, 384), F32),
        ),
        in_specs=[vmem()] * 6,
        out_specs=(vmem(),) * 5,
        scratch_shapes=[
            pltpu.VMEM((128, 128), F32),
            pltpu.VMEM((128, 512), F32),
            pltpu.VMEM((128, 512), F32),
            pltpu.VMEM((128, 512), F32),
            pltpu.VMEM((8, 128), F32),
            pltpu.VMEM((16, 8, 128), F32),
            sem((16,)), sem((16,)),
        ],
        compiler_params=params(1),
        name="mix",
    )(*args)


def small_steps(grads, half, total, slots, own, full, c_send, c_recv, s_send, s_recv, g_send, g_recv, e_send, e_recv):
    x_hi, y, core, x_lo, z = coords()
    chip = x_hi * 4 + y
    partner = core_peer()

    def to_chip(j):
        return ((x_hi + j // 4) % 2) * 4 + (y + j % 4) % 4

    def swap():
        return remote(grads.at[1 - core], half, c_send, c_recv, partner)

    def scatter(j):
        return remote(total.at[to_chip(j)], slots.at[chip], s_send.at[j], s_recv.at[j], chip_peer(j))

    def gather(j):
        return remote(own, full.at[core, chip], g_send.at[j], g_recv.at[j], chip_peer(j))

    def share():
        return remote(full.at[core], full.at[core], e_send, e_recv, partner)

    swap().start()
    yield
    swap().wait()
    total[...] = grads[core] + half[...]
    for j in range(1, 8):
        scatter(j).start()
    slots[chip] = total[chip]
    yield
    for j in range(1, 8):
        scatter(j).wait()
    result = slots[0]
    for i in range(1, 8):
        result = result + slots[i]
    own[...] = result
    for j in range(1, 8):
        gather(j).start()
    full[core, chip] = result
    yield
    for j in range(1, 8):
        gather(j).wait()
    share().start()
    yield
    share().wait()


def small_scratch():
    sem = pltpu.SemaphoreType.DMA
    return [
        pltpu.VMEM((2, 8, 40, 384), F32),
        pltpu.VMEM((8, 40, 384), F32),
        pltpu.VMEM((8, 40, 384), F32),
        pltpu.VMEM((8, 40, 384), F32),
        pltpu.VMEM((40, 384), F32),
        pltpu.VMEM((2, 8, 40, 384), F32),
        sem, sem, sem((8,)), sem((8,)), sem((8,)), sem((8,)), sem, sem,
    ]


def output_kernel(
    normed, gate_low, value_low, backs, small, tok, tokc, upc, wcat, wof, s_in, s_out, s_step,
    layer_out, input_grad, grad_gate, grad_value, grad_output, grad_in, grad_out, grad_step, grad_small,
    all_n, all_g, all_v, part_l, part_d, side, low, g_send, g_recv, grads, grads_in, h_send, h_recv, *scratch,
):
    x_hi, y, core, x_lo, z = coords()
    chip = x_hi * 4 + y
    for_total, scratch = scratch[:8], scratch[8:]
    for_small, scratch = scratch[:14], scratch[14:]
    for_layer, scratch = scratch[:12], scratch[12:]
    for_input, scratch = scratch[:12], scratch[12:]
    gather_layer, gather_input = scratch[:4], scratch[4:]
    partner = core_peer()
    turned, turner, stays = turn_peers()
    devices = [chip_peer(j) for j in range(1, 8)] + [partner] + [tensor_peer(j) for j in range(1, 16)]
    announce(devices)

    @pl.when(jnp.logical_not(stays))
    def _():
        announce([turned, turner])

    gathered(len(devices) + jnp.where(stays, 0, 2))
    sources = (normed, gate_low, value_low)
    targets = (all_n, all_g, all_v)

    def copy(i, j):
        return remote(sources[i], targets[i].at[chip], g_send.at[i, j], g_recv.at[i, j], chip_peer(j))

    for j in range(1, 8):
        copy(0, j).start()
    back_part, back_full = for_total[0], for_total[7]
    back_part[...] = backs[...].reshape(16, 8, 384)
    back_steps = total_steps(back_part, for_total[1], for_total[2], back_full, *for_total[3:7])
    drive(back_steps)
    for i in range(3):
        targets[i][chip] = sources[i][...]
    for j in range(1, 8):
        copy(0, j).wait_recv()
    for i in (1, 2):
        for j in range(1, 8):
            copy(i, j).start()

    def store(part, index, block):
        row = 2 * ((y + 4 - index % 4) % 4)
        part[row, index // 4] = block[:, :512]
        part[row + 1, index // 4] = block[:, 512:]

    def out_block(index, carry):
        store(part_l, index, dot_cols(all_n[index], wof[...]))
        return carry

    lax.fori_loop(0, 8, out_block, 0)
    layer_steps = reduce_steps(part_l, *for_layer)
    drive(layer_steps)
    drive(back_steps)

    theirs = pl.ds(pl.multiple_of((1 - core) * 512, 512), 512)
    mine = pl.ds(pl.multiple_of(core * 512, 512), 512)

    def grad_copy(i):
        return remote(grads.at[i, theirs], grads_in.at[i], h_send.at[i], h_recv.at[i], partner)

    def weight_grad(i, left, right):
        def rows(index, carry):
            at = pl.ds(pl.multiple_of(index * 256, 256), 256)
            grads[i, at, :] = dot_rows(left[:, :, at].reshape(1024, 256), right[...].reshape(1024, 512))
            return carry

        lax.fori_loop(0, 4, rows, 0)
        grad_copy(i).start()

    drive(layer_steps)
    weight_grad(0, upc, all_n)
    drive(layer_steps)
    finish(back_steps)
    low[...] = back_full[...].reshape(128, 384).astype(BF16)
    side[...] = (
        dot_cols(low[:, 0:128], s_in[...]) + dot_cols(low[:, 128:256], s_out[...])
        + dot_cols(low[:, 256:384], s_step[...])
    )
    slab = tok[:, pl.ds(pl.multiple_of((x_lo * 8 + z) * 512, 512), 512)]
    state_grads = jnp.concatenate(
        [dot_rows(slab, low[...]), small[...], jnp.zeros((112, 384), F32)], axis=0
    )
    for_small[0][...] = state_grads.reshape(2, 8, 40, 384)
    sum_steps = small_steps(*for_small)
    drive(sum_steps)
    drive(layer_steps)

    for i in (1, 2):
        for j in range(1, 8):
            copy(i, j).wait_recv()

    def dense_block(index, carry):
        store(
            part_d, index, dot_cols(all_g[index], wcat[:, 0:512]) + dot_cols(all_v[index], wcat[:, 512:1024])
        )
        return carry

    lax.fori_loop(0, 8, dense_block, 0)
    input_steps = reduce_steps(part_d, *for_input)
    drive(input_steps)
    drive(layer_steps)
    drive(sum_steps)
    drive(input_steps)
    drive(layer_steps)
    drive(sum_steps)
    drive(input_steps)
    finish(layer_steps)

    def blocks_of(result):
        def block(at_side, level):
            return result.at[:, pl.ds(pl.multiple_of((at_side * 8 + level) * 512, 512), 512)]

        return block

    own = pl.ds(pl.multiple_of((x_lo * 8 + z) * 512, 512), 512)
    layer_out[:, own] = for_layer[9][...]
    layer_gather = gather_steps(blocks_of(layer_out), *gather_layer)
    drive(layer_gather)
    weight_grad(1, tokc, all_g)
    drive(input_steps)
    drive(layer_gather)
    drive(sum_steps)
    drive(input_steps)
    drive(layer_gather)
    drive(input_steps)
    drive(layer_gather)
    weight_grad(2, tokc, all_v)
    finish(input_steps)
    input_grad[:, own] = (for_input[9][...] + side[...]).astype(BF16)
    input_gather = gather_steps(blocks_of(input_grad), *gather_input)
    drive(input_gather)
    finish(layer_gather)
    finish(sum_steps)
    summed = for_small[5][...].reshape(640, 384)
    grad_in[...] = summed[0:512, 0:128]
    grad_out[...] = summed[0:512, 128:256]
    grad_step[...] = summed[0:512, 256:384]
    grad_small[...] = summed[512:528, :]
    drive(input_gather)
    outs = (grad_output, grad_gate, grad_value)
    for i in range(2):
        grad_copy(i).wait_recv()
        outs[i][...] = grads[i, mine, :] + grads_in[i]
    drive(input_gather)
    grad_copy(2).wait_recv()
    grad_value[...] = grads[2, mine, :] + grads_in[2]
    finish(input_gather)
    for i in range(3):
        grad_copy(i).wait_send()
        for j in range(1, 8):
            copy(i, j).wait_send()


def outputs(*args):
    sem = pltpu.SemaphoreType.DMA
    return pl.pallas_call(
        output_kernel,
        out_shape=(
            jax.ShapeDtypeStruct((128, 8192), BF16),
            jax.ShapeDtypeStruct((128, 8192), BF16),
            jax.ShapeDtypeStruct((512, 512), F32),
            jax.ShapeDtypeStruct((512, 512), F32),
            jax.ShapeDtypeStruct((512, 512), F32),
            jax.ShapeDtypeStruct((512, 128), F32),
            jax.ShapeDtypeStruct((512, 128), F32),
            jax.ShapeDtypeStruct((512, 128), F32),
            jax.ShapeDtypeStruct((16, 384), F32),
        ),
        in_specs=[vmem()] * 13,
        out_specs=(vmem(),) * 9,
        scratch_shapes=[
            pltpu.VMEM((8, 128, 512), BF16),
            pltpu.VMEM((8, 128, 512), BF16),
            pltpu.VMEM((8, 128, 512), BF16),
            pltpu.VMEM((8, 2, 128, 512), F32),
            pltpu.VMEM((8, 2, 128, 512), F32),
            pltpu.VMEM((128, 512), F32),
            pltpu.VMEM((128, 384), BF16),
            sem((3, 8)), sem((3, 8)),
            pltpu.VMEM((3, 1024, 512), F32),
            pltpu.VMEM((3, 512, 512), F32),
            sem((3,)), sem((3,)),
        ]
        + total_scratch() + [pltpu.VMEM((16, 8, 384), F32)]
        + small_scratch() + reduce_scratch(BF16) + reduce_scratch(F32) + gather_scratch() * 2,
        compiler_params=params(2),
        cost_estimate=pl.CostEstimate(flops=6 * 10**9, bytes_accessed=300 * 10**6, transcendentals=0),
        name="outputs",
    )(*args)


def per_device(
    tokens_in, proj_gate, proj_value, state_in, state_out, proj_step,
    step_bias, decay_log, skip_scale, norm_gain, proj_output, upstream,
):
    tokc, upc, wcat, wof, gate, value, gn, state = project(
        tokens_in, upstream, proj_gate, proj_value, proj_output, state_in, state_out, proj_step
    )
    heads = jnp.pad(jnp.stack([step_bias, decay_log, skip_scale], axis=1), ((0, 0), (0, 125)))
    normed, gate_low, value_low, backs, small = mix(gate, value, gn, state, heads, norm_gain.reshape(1, 512))
    (
        layer_out, input_grad, grad_gate, grad_value, grad_output,
        grad_state_in, grad_state_out, grad_step, sums,
    ) = outputs(
        normed, gate_low, value_low, backs, small, tokens_in, tokc, upc, wcat, wof, state_in, state_out, proj_step
    )
    grad_gain = jnp.concatenate([sums[0], sums[1, :128]])
    grad_skip = jnp.concatenate([sums[2], sums[3, :128]]).reshape(8, 64).sum(axis=1)
    return (
        layer_out, input_grad, grad_gate, grad_value, grad_output,
        grad_state_in, grad_state_out, grad_step, sums[8:16, 0], sums[8:16, 1], grad_skip, grad_gain,
    )


def solution(mesh):
    block = P("dp", "tensor")
    rows = P("dp", None)
    slab = P("tensor", None)
    vector = P("tensor")
    return jax.shard_map(
        per_device,
        mesh=mesh,
        in_specs=(rows, block, block, slab, slab, slab, vector, vector, vector, vector, block, rows),
        out_specs=(rows, rows, block, block, block, slab, slab, slab, vector, vector, vector, vector),
        check_vma=False,
    )
```

time: 909 us -> 292 us (0.32)
  waiting for transfers between devices: 607 us -> 0 us
  Pallas kernels: 0 us -> 272 us
  blocking collectives: 170 us -> 0 us
  matrix products: 83.4 us -> 0 us
  between operations: 16.2 us -> 0.68 us
    pallas_call x0 -> x3, Pallas kernels: none -> 272 us  [the longest x1 149 us: outputs(): pl.pallas_call(output_kernel, out_shape=(jax.ShapeDtypeStruct((128, 8192)...]
    reduce_scatter x3 -> x0, waiting for transfers between devices: 241 us -> none  [the longest x1 241 us: per_device(): lax.psum_scatter(contract_rows(piece, grad_both), 'dp', scatter_dimension...]
    all_gather x5 -> x0, waiting for transfers between devices: 203 us -> none  [the longest x1 77.7 us: per_device(): side_all = lax.all_gather(side_back, 'tensor', axis=1, tiled=True)]
    psum x4 -> x0, blocking collectives: 170 us -> none  [the longest x1 62.3 us: per_device(): sum_b, sum_c, sum_step = lax.psum((back_b, back_c, step_padded), 'tensor')]
    psum x3 -> x0, waiting for transfers between devices: 162 us -> none  [the longest x1 132 us: per_device(): lax.psum((jnp.dot(feature_slab, state_in, preferred_element_type=f32), jn...]
    dot_general x23 -> x0, matrix products: 83.4 us -> none  [the longest x5 31.8 us: contract_rows(): lax.dot_general(left, right, (((0,), (0,)), ((), ())), preferred_element_...]
  transfers between devices with their start and end apart: 11 -> 0, of which waited for: 7 -> 0; matrix products, arithmetic and copies ran while one was open for 10% -> 0% of each run, Pallas kernels for 0% -> 0%
where the time goes in v1:
time: 292 us; the launch traced here: 291 us
  Pallas kernels  272 us (93%)
  local copies, waits for them, and re-layouts  16.2 us (6%)
    pallas_call x1, Pallas kernels, outputs(): pl.pallas_call(output_kernel, out_shape=(jax.ShapeDtypeStruct((128, 8192)...  149 us
    pallas_call x1, Pallas kernels, project(): pl.pallas_call(project_kernel, out_shape=(jax.ShapeDtypeStruct((8, 128, 1...  111 us
    pallas_call x1, Pallas kernels, mix(): pl.pallas_call(mix_kernel, out_shape=(jax.ShapeDtypeStruct((128, 512), BF...  12.5 us
    unnamed x22, local copies, waits for them, and re-layouts  10.9 us

profile of v1, /device:TPU:2, one launch (start us, length us, event | category | flops | bytes accessed | tf_op | source)
XLA Modules:
  0.0 291.2 jit_solution(13007719919960513907)
XLA Ops:
  0.6 0.7 copy.30
  1.4 0.7 copy.31
  2.1 0.7 copy.32
  2.8 0.7 select_maximum_fusion.heads
  3.5 111.1 %project.1 = (bf16[8,128,1024]{2,1,0:T(8,128)(2,1)}, bf16[8,128,1024]{2,1,0:T(8,128)(2,1)}, bf16[1024,1024]{1,0:T(8,128)(2,1)}, bf16[1024,512]{1,0:T(8,128)(2,1)...) custom-call(bf16[128,8192]{1,0:T(8,128)(2,1)} %tok.3, ...), custom_call_target="tpu_custom_call" | custom-call | flops 3000000000 | bytes 200000000 | tf_op jit(solution)/shard_map/project/pallas_call | solution.py:494
  114.6 12.5 %mix.1 = (bf16[128,512]{1,0:T(8,128)(2,1)}, bf16[128,512]{1,0:T(8,128)(2,1)}, bf16[128,512]{1,0:T(8,128)(2,1)}, f32[128,384]{1,0:T(8,128)}, f32[16,384]{1,0:T(8,128)}) custom-call(f32[128,512]{1,0:T(8,128)} %get-tuple-element.34.gate, f32[128,512]{1,0:T(8,128)} %get-tuple-element.35.value, f32[128,512]{1,0:T(8,128)} %get-tuple-element.36.gn, ...), custom_call_target="tpu_custom_call" | custom-call | tf_op jit(solution)/shard_map/mix/pallas_call | solution.py:652
  127.1 148.8 %outputs.1 = (bf16[128,8192]{1,0:T(8,128)(2,1)}, bf16[128,8192]{1,0:T(8,128)(2,1)}, f32[512,512]{1,0:T(8,128)}, f32[512,512]{1,0:T(8,128)}, f32[512,512]{1,0:T(8...) custom-call(bf16[128,512]{1,0:T(8,128)(2,1)} %get-tuple-element.38.normed, ...), custom_call_target="tpu_custom_call" | custom-call | flops 6000000000 | bytes 300000000 | tf_op jit(solution)/shard_map/outputs/pallas_call | solution.py:892
  275.9 0.8 slice_bitcast_fusion
  276.7 1.5 slice_reduce_fusion
  278.2 0.8 slice_reduce_fusion.2
  279.0 0.6 pad_maximum_fusion
  279.6 0.1 reshape.31
  279.6 0.6 reduce_sum.9
  280.3 3.2 %copy.41 = bf16[128,8192]{1,0:T(8,128)(2,1)} copy(bf16[128,8192]{1,0:T(8,128)(2,1)} %get-tuple-element.76) | data formatting | bytes 4194304
  283.5 0.0 copy-done
  283.5 1.3 copy.42
  284.8 0.6 copy-done.3
  285.5 1.0 copy.43
  286.5 0.6 copy-done.2
  287.1 1.0 copy.44
  288.1 1.0 copy.45
  289.0 0.7 copy.46
  289.7 0.7 copy.47
  290.5 0.7 copy.48
  (11 shorter events, 0.0 us)
Async XLA Ops:
  280.3 3.2 %copy-start = (bf16[128,8192]{1,0:T(8,128)(2,1)S(1)}, bf16[128,8192]{1,0:T(8,128)(2,1)}, u32[]{:S(2)}) copy-start(bf16[128,8192]{1,0:T(8,128)(2,1)} %get-tuple-element.77) | copy-start | bytes 6291460
  283.5 2.0 copy-start.3
  285.5 1.6 copy-start.2
  285.5 2.6 copy-start.1
  287.1 2.0 copy-start.6
  287.1 2.7 copy-start.5
  288.1 2.4 copy-start.4

commit v2 on v1

--- a/solution.py
+++ b/solution.py
@@ -11,7 +11,7 @@
 INNER = 8192
 F32 = jnp.float32
 BF16 = jnp.bfloat16
-VMEM_LIMIT = 58 * 2**20
+VMEM_LIMIT = 60 * 2**20
 
 
 def coords():
@@ -138,28 +138,43 @@
     ]
 
 
-def gather_steps(block, a_send, a_recv, b_send, b_recv):
-    x_hi, y, core, x_lo, z = coords()
-    up = place(x_hi, y, core, x_lo, (z + 1) % 8)
-    down = place(x_hi, y, core, x_lo, (z + 7) % 8)
-    across = place(x_hi, y, core, 1 - x_lo, z)
-    own = block(x_lo, z)
+def along_z():
+    x_hi, y, core, x_lo, z = coords()
+    return (
+        8, z, x_lo, place(x_hi, y, core, x_lo, (z + 1) % 8), place(x_hi, y, core, x_lo, (z + 7) % 8),
+        place(x_hi, y, core, 1 - x_lo, z),
+    )
+
+
+def along_y():
+    x_hi, y, core, x_lo, z = coords()
+    return (
+        4, y, x_hi, place(x_hi, (y + 1) % 4, core, x_lo, z), place(x_hi, (y + 3) % 4, core, x_lo, z),
+        place(1 - x_hi, y, core, x_lo, z),
+    )
+
+
+def gather_steps(ring, block, a_send, a_recv, b_send, b_recv):
+    size, here, side, up, down, across = ring
+    count = size // 2
+    own = block(side, here)
     cross = remote(own, own, a_send, a_recv, across)
     cross.start()
 
     def copy(way, step, other):
-        level = (z + 8 - step) % 8 if way == 0 else (z + step) % 8
-        ref = block(1 - x_lo if other else x_lo, level)
+        level = (here + size - step) % size if way == 0 else (here + step) % size
+        ref = block(1 - side if other else side, level)
         return remote(
             ref, ref, b_send.at[way, step, other], b_recv.at[way, step, other], up if way == 0 else down
         )
 
     def goes(way, step, other):
-        return step < 3 or other == way
-
-    for step in range(4):
+        return step < count - 1 or other == way
+
+    for step in range(count):
         for other in (0, 1):
             if step == 0 and other == 1:
+                yield
                 cross.wait_recv()
             for way in (0, 1):
                 if step > 0:
@@ -167,19 +182,61 @@
                 if goes(way, step, other):
                     copy(way, step, other).start()
         yield
-    copy(0, 3, 0).wait_recv()
-    copy(1, 3, 1).wait_recv()
+    copy(0, count - 1, 0).wait_recv()
+    copy(1, count - 1, 1).wait_recv()
     cross.wait_send()
-    for step in range(4):
+    for step in range(count):
         for other in (0, 1):
             for way in (0, 1):
                 if goes(way, step, other):
                     copy(way, step, other).wait_send()
 
 
-def gather_scratch():
+def gather_scratch(count):
     sem = pltpu.SemaphoreType.DMA
-    return [sem, sem, sem((2, 4, 2)), sem((2, 4, 2))]
+    return [sem, sem, sem((2, count, 2)), sem((2, count, 2))]
+
+
+def gather_last_across(array, d_send, d_recv, x_send, x_recv):
+    x_hi, y, core, x_lo, z = coords()
+    ways = (place(x_hi, (y + 1) % 4, core, x_lo, z), place(x_hi, (y + 3) % 4, core, x_lo, z))
+    across = place(1 - x_hi, y, core, x_lo, z)
+
+    def near(way):
+        ref = array.at[x_hi * 4 + y]
+        return remote(ref, ref, d_send.at[way, 0], d_recv.at[way, 0], ways[way])
+
+    def far(way):
+        ref = array.at[x_hi * 4 + (y + 3 + 2 * way) % 4, pl.ds(64 * way, 64)]
+        return remote(ref, ref, d_send.at[way, 1], d_recv.at[way, 1], ways[way])
+
+    def cross(i):
+        ref = array.at[x_hi * 4 + (y + i) % 4]
+        return remote(ref, ref, x_send.at[i], x_recv.at[i], across)
+
+    for way in (0, 1):
+        near(way).start()
+    cross(0).start()
+    yield
+    for way in (0, 1):
+        near(way).wait_recv()
+        far(way).start()
+        cross(3 - 2 * way).start()
+    yield
+    for way in (0, 1):
+        far(way).wait_recv()
+    cross(2).start()
+    yield
+    for i in range(4):
+        cross(i).wait()
+    for way in (0, 1):
+        near(way).wait_send()
+        far(way).wait_send()
+
+
+def last_across_scratch():
+    sem = pltpu.SemaphoreType.DMA
+    return [sem((2, 2)), sem((2, 2)), sem((4,)), sem((4,))]
 
 
 def turn_peers():
@@ -192,48 +249,64 @@
 
 def reduce_steps(part, outbox, inbox, send, recv, xbox, xin, x_send, x_recv, tbox, tin, t_send, t_recv):
     x_hi, y, core, x_lo, z = coords()
-    up = place(x_hi, y, core, x_lo, (z + 1) % 8)
-    down = place(x_hi, y, core, x_lo, (z + 7) % 8)
+    ways = (place(x_hi, y, core, x_lo, (z + 1) % 8), place(x_hi, y, core, x_lo, (z + 7) % 8))
     across = place(x_hi, y, core, 1 - x_lo, z)
     turned, turner, stays = turn_peers()
-
-    def copy(way, step, block):
-        return remote(
-            outbox.at[way, step, block], inbox.at[way, step, block],
-            send.at[way, step, block], recv.at[way, step, block], up if way == 0 else down,
-        )
-
-    def goes(way, step, block):
-        return step > 0 or block == way
-
-    for step in range(4):
-        for block in (0, 1):
-            for way in (0, 1):
-                if not goes(way, step, block):
-                    continue
-                target = (z + 4 - step) % 8 if way == 0 else (z + 4 + step) % 8
-                value = part[target, block]
-                if step > 0 and goes(way, step - 1, block):
-                    copy(way, step - 1, block).wait_recv()
-                    value = value + inbox[way, step - 1, block].astype(F32)
-                outbox[way, step, block] = value.astype(BF16)
-                copy(way, step, block).start()
-        yield
-    for block in (0, 1):
-        for way in (0, 1):
-            copy(way, 3, block).wait_recv()
-        part[z, block] = part[z, block] + (inbox[0, 3, block].astype(F32) + inbox[1, 3, block].astype(F32))
-    xbox[...] = part[z, 1 - x_lo].astype(BF16)
-    cross = remote(xbox, xin, x_send, x_recv, across)
-    cross.start()
-    yield
-    for step in range(4):
-        for block in (0, 1):
-            for way in (0, 1):
-                if goes(way, step, block):
-                    copy(way, step, block).wait_send()
-    cross.wait()
-    tbox[...] = (part[z, x_lo] + xin[...].astype(F32)).astype(tbox.dtype)
+    other = 1 - x_lo
+
+    def level(way, distance):
+        return (z + distance) % 8 if way == 0 else (z + 8 - distance) % 8
+
+    def copy(way, i):
+        at = (way, i, pl.ds(64 * way, 64)) if i == 2 else (way, i)
+        return remote(outbox.at[at], inbox.at[at], send.at[way, i], recv.at[way, i], ways[way])
+
+    def cross(i):
+        return remote(xbox.at[i], xin.at[i], x_send.at[i], x_recv.at[i], across)
+
+    def received(way, i):
+        copy(way, i).wait_recv()
+        return inbox[way, i].astype(F32)
+
+    def push(way, i, value):
+        outbox[way, i] = value.astype(BF16)
+        copy(way, i).start()
+
+    xbox[0] = part[(z + 4) % 8, other].astype(BF16)
+    cross(0).start()
+    for way in (0, 1):
+        push(way, 0, part[level(way, 3), other])
+    xbox[3] = part[z, other].astype(BF16)
+    cross(3).start()
+    yield
+    cross(0).wait_recv()
+    far = (part[(z + 4) % 8, x_lo] + xin[0].astype(F32)).astype(BF16)
+    for way in (0, 1):
+        outbox[way, 2, 64 * way : 64 * way + 64, :] = far[64 * way : 64 * way + 64, :]
+        copy(way, 2).start()
+    for way in (0, 1):
+        push(way, 1, part[level(way, 2), other] + received(way, 0))
+    yield
+    for way in (0, 1):
+        copy(way, 2).wait_recv()
+        rows = slice(64 * way, 64 * way + 64)
+        at = level(way, 3)
+        part[at, x_lo, rows, :] = part[at, x_lo, rows, :] + inbox[way, 2, rows, :].astype(F32)
+        push(way, 3, part[at, x_lo])
+    for way in (0, 1):
+        xbox[1 + way] = (part[level(way, 1), other] + received(way, 1)).astype(BF16)
+        cross(1 + way).start()
+    yield
+    for way in (0, 1):
+        push(way, 4, part[level(way, 2), x_lo] + received(way, 3))
+    yield
+    for way in (0, 1):
+        cross(1 + way).wait_recv()
+        push(way, 5, part[level(way, 1), x_lo] + xin[1 + way].astype(F32) + received(way, 4))
+    yield
+    cross(3).wait_recv()
+    home = part[z, x_lo] + xin[3].astype(F32)
+    tbox[...] = (home + (received(0, 5) + received(1, 5))).astype(tbox.dtype)
     turn = remote(tbox, tin, t_send, t_recv, turned)
 
     @pl.when(stays)
@@ -244,6 +317,11 @@
     def _():
         turn.start()
 
+    for way in (0, 1):
+        for i in range(6):
+            copy(way, i).wait_send()
+    for i in range(4):
+        cross(i).wait_send()
     yield
 
     @pl.when(jnp.logical_not(stays))
@@ -254,16 +332,80 @@
 def reduce_scratch(kind):
     sem = pltpu.SemaphoreType.DMA
     return [
-        pltpu.VMEM((2, 4, 2, 128, 512), BF16),
-        pltpu.VMEM((2, 4, 2, 128, 512), BF16),
-        sem((2, 4, 2)), sem((2, 4, 2)),
-        pltpu.VMEM((128, 512), BF16),
-        pltpu.VMEM((128, 512), BF16),
-        sem, sem,
+        pltpu.VMEM((2, 6, 128, 512), BF16),
+        pltpu.VMEM((2, 6, 128, 512), BF16),
+        sem((2, 6)), sem((2, 6)),
+        pltpu.VMEM((4, 128, 512), BF16),
+        pltpu.VMEM((4, 128, 512), BF16),
+        sem((4,)), sem((4,)),
         pltpu.VMEM((128, 512), kind),
         pltpu.VMEM((128, 512), kind),
         sem, sem,
     ]
+
+
+def spread_steps(block, z_send, z_recv, x_send, x_recv):
+    x_hi, y, core, x_lo, z = coords()
+    ways = (place(x_hi, y, core, x_lo, (z + 1) % 8), place(x_hi, y, core, x_lo, (z + 7) % 8))
+    across = place(x_hi, y, core, 1 - x_lo, z)
+
+    def level(way, distance):
+        return (z + 8 - distance) % 8 if way == 0 else (z + distance) % 8
+
+    def copy(way, i):
+        if i < 3:
+            ref = block(x_lo, level(way, i), None)
+        elif i == 3:
+            ref = block(x_lo, level(way, 3), way)
+        else:
+            ref = block(1 - x_lo, level(way, i - 3), None)
+        return remote(ref, ref, z_send.at[way, i], z_recv.at[way, i], ways[way])
+
+    def cross(i):
+        ref = block(x_lo, (z, level(0, 1), level(1, 1), (z + 4) % 8)[i], None)
+        return remote(ref, ref, x_send.at[i], x_recv.at[i], across)
+
+    for way in (0, 1):
+        copy(way, 0).start()
+    cross(0).start()
+    yield
+    for way in (0, 1):
+        copy(way, 0).wait_recv()
+        copy(way, 1).start()
+        cross(1 + way).start()
+    yield
+    for way in (0, 1):
+        copy(way, 1).wait_recv()
+        copy(way, 2).start()
+    for way in (0, 1):
+        cross(1 + way).wait_recv()
+        copy(way, 4).start()
+    yield
+    for way in (0, 1):
+        copy(way, 2).wait_recv()
+        copy(way, 3).start()
+    for way in (0, 1):
+        copy(way, 4).wait_recv()
+        copy(way, 5).start()
+    yield
+    for way in (0, 1):
+        copy(way, 3).wait_recv()
+    cross(3).start()
+    yield
+    for way in (0, 1):
+        copy(way, 5).wait_recv()
+    cross(0).wait_recv()
+    cross(3).wait_recv()
+    for way in (0, 1):
+        for i in range(6):
+            copy(way, i).wait_send()
+    for i in range(4):
+        cross(i).wait_send()
+
+
+def spread_scratch():
+    sem = pltpu.SemaphoreType.DMA
+    return [sem((2, 6)), sem((2, 6)), sem((4,)), sem((4,))]
 
 
 def rows_first(part, result, inbox, send, recv, xin, x_send, x_recv):
@@ -380,12 +522,13 @@
 
 def project_kernel(
     tok, up, wg, wv, wo, s_in, s_out, s_step,
-    tokc, upc, wcat, wof, gate, value, gn, state,
-    part_g, part_v, part_n, w_send, w_recv, t_send, t_recv, u_send, u_recv, *scratch,
+    tokc, upc, wcat, wof, gate, value, gn, state, slab_out,
+    part_g, part_v, part_n, w_send, w_recv, p_send, p_recv, f_send, f_recv, *scratch,
 ):
     x_hi, y, core, x_lo, z = coords()
     chip = x_hi * 4 + y
     for_state, scratch = scratch[:7], scratch[7:]
+    for_tokens, scratch = scratch[:4], scratch[4:]
     for_upstream, scratch = scratch[:4], scratch[4:]
     for_gate, scratch = scratch[:6], scratch[6:]
     for_value, for_normed = scratch[:6], scratch[6:]
@@ -399,13 +542,43 @@
     partner = core_peer()
     devices = [chip_peer(j) for j in range(1, 8)] + [partner] + [tensor_peer(j) for j in range(1, 16)]
     announce(devices)
-    slab = tok[:, pl.ds(pl.multiple_of((x_lo * 8 + z) * 512, 512), 512)]
-    state_part = for_state[0]
-    for i, weights in enumerate((s_in, s_out, s_step)):
-        state_part[:, :, 128 * i : 128 * i + 128] = dot(slab, weights[...]).reshape(16, 8, 128)
     gathered(len(devices))
-
     mine = pl.ds(pl.multiple_of(core * 512, 512), 512)
+
+    rows = pl.ds(pl.multiple_of(z * 16, 16), 16)
+    side = pl.ds(pl.multiple_of(512 + x_lo * 256, 256), 256)
+    direct = pl.ds(0, 512)
+    sources, arrays = (tok, up), (tokc, upc)
+
+    def part_copy(i, j):
+        columns = pl.ds(pl.multiple_of(to_chip(j) * 1024 + 512 + x_lo * 256, 256), 256)
+        return remote(
+            sources[i].at[rows, columns], arrays[i].at[chip, rows, side], p_send.at[i, j], p_recv.at[i, j], chip_peer(j)
+        )
+
+    def full_copy(i, j):
+        columns = pl.ds(pl.multiple_of(to_chip(j) * 1024, 1024), 512)
+        return remote(
+            sources[i].at[:, columns], arrays[i].at[chip, :, direct], f_send.at[i, j], f_recv.at[i, j], chip_peer(j)
+        )
+
+    def keep(i):
+        arrays[i][chip, :, direct] = sources[i][:, pl.ds(pl.multiple_of(chip * 1024, 1024), 512)]
+        own = pl.ds(pl.multiple_of(chip * 1024 + 512 + x_lo * 256, 256), 256)
+        arrays[i][chip, rows, side] = sources[i][rows, own]
+
+    def shared(array):
+        def block(at_side, level):
+            columns = pl.ds(pl.multiple_of(512 + at_side * 256, 256), 256)
+            return array.at[:, pl.ds(pl.multiple_of(level * 16, 16), 16), columns]
+
+        return block
+
+    for j in range(1, 8):
+        part_copy(0, j).start()
+    for j in range(1, 8):
+        full_copy(0, j).start()
+    keep(0)
     w_copies = []
     for i, (src, dst) in enumerate(
         ((wg, wcat.at[mine, pl.ds(0, 512)]), (wv, wcat.at[mine, pl.ds(512, 512)]), (wo, wof.at[mine, :]))
@@ -413,76 +586,72 @@
         copy = remote(src, dst, w_send.at[i], w_recv.at[i], partner)
         copy.start()
         w_copies.append(copy)
-
-    rows = pl.ds(pl.multiple_of(z * 16, 16), 16)
-    side = pl.ds(pl.multiple_of(x_lo * 512, 512), 512)
-
-    def up_copy(j):
-        columns = pl.ds(pl.multiple_of(to_chip(j) * 1024 + x_lo * 512, 512), 512)
-        return remote(up.at[rows, columns], upc.at[chip, rows, side], u_send.at[j], u_recv.at[j], chip_peer(j))
-
-    def tok_copy(j):
-        columns = pl.ds(pl.multiple_of(to_chip(j) * 1024, 1024), 1024)
-        return remote(tok.at[:, columns], tokc.at[chip], t_send.at[j], t_recv.at[j], chip_peer(j))
-
     for j in range(1, 8):
-        up_copy(j).start()
-    state_steps = total_steps(state_part, for_state[1], for_state[2], state, *for_state[3:])
-    drive(state_steps)
+        part_copy(0, j).wait()
+    tok_steps = gather_steps(along_z(), shared(tokc), *for_tokens)
+    drive(tok_steps)
     for j in range(1, 8):
-        tok_copy(j).start()
-
+        part_copy(1, j).start()
+    slab = tok[:, pl.ds(pl.multiple_of((x_lo * 8 + z) * 512, 512), 512)]
+    slab_out[...] = slab
+    state_part = for_state[0]
+    for i, weights in enumerate((s_in, s_out, s_step)):
+        state_part[:, :, 128 * i : 128 * i + 128] = dot(slab, weights[...]).reshape(16, 8, 128)
+    drive(tok_steps)
+    keep(1)
     wcat[mine, pl.ds(0, 512)] = wg[...]
     wcat[mine, pl.ds(512, 512)] = wv[...]
     wof[mine, :] = wo[...]
-    tokc[chip] = tok[:, pl.ds(pl.multiple_of(chip * 1024, 1024), 1024)]
-    upc[chip, rows, side] = up[rows, pl.ds(pl.multiple_of(chip * 1024 + x_lo * 512, 512), 512)]
+    drive(tok_steps)
     for j in range(1, 8):
-        up_copy(j).wait()
-
-    def up_block(at_side, level):
-        return upc.at[
-            :, pl.ds(pl.multiple_of(level * 16, 16), 16), pl.ds(pl.multiple_of(at_side * 512, 512), 512)
-        ]
-
-    up_steps = gather_steps(up_block, *for_upstream)
+        part_copy(1, j).wait()
+    drive(tok_steps)
+    for j in range(1, 8):
+        full_copy(1, j).start()
+    up_steps = gather_steps(along_z(), shared(upc), *for_upstream)
     drive(up_steps)
-    drive(state_steps)
     for copy in w_copies:
         copy.wait()
-    drive(up_steps, 2)
-
-    def multiply(src):
-        part_g[src] = dot(tokc[src], wcat[:, 0:512])
-        part_v[src] = dot(tokc[src], wcat[:, 512:1024])
-
-    multiply(chip)
-
-    def serve(j, carry):
-        tok_copy(j).wait()
-        multiply(from_chip(j))
-        return carry
-
-    lax.fori_loop(1, 8, serve, 0)
+    drive(tok_steps)
+    finish(tok_steps)
+    drive(up_steps)
+    for j in range(1, 8):
+        full_copy(0, j).wait()
+
+    def multiply(part, tokens, weights, start):
+        def columns(n, carry):
+            at = pl.ds(pl.multiple_of(n * 256, 256), 256)
+            weight = weights[:, pl.ds(pl.multiple_of(start + n * 256, 256), 256)]
+            part[:, :, at] = dot(tokens[...].reshape(1024, 1024), weight).reshape(8, 128, 256)
+            return carry
+
+        lax.fori_loop(0, 2, columns, 0)
+
     gate_steps = across_first(part_g, gate, *for_gate)
     value_steps = rows_first(part_v, value, *for_value)
+    normed_steps = rows_first(part_n, gn, *for_normed)
+    multiply(part_g, tokc, wcat, 0)
+    drive(gate_steps)
+    multiply(part_v, tokc, wcat, 512)
+    drive(value_steps)
+    drive(up_steps)
+    state_steps = total_steps(state_part, for_state[1], for_state[2], state, *for_state[3:])
+    drive(state_steps)
+    drive(up_steps)
+    drive(value_steps)
+    drive(up_steps)
+    finish(up_steps)
+    for j in range(1, 8):
+        full_copy(1, j).wait()
+    multiply(part_n, upc, wof, 0)
+    drive(normed_steps)
+    drive(gate_steps)
+    drive(state_steps)
+    drive(normed_steps)
+    drive(gate_steps)
     drive(value_steps)
     drive(gate_steps)
-    finish(up_steps)
-
-    def serve_upstream(src, carry):
-        part_n[src] = dot(upc[src], wof[...])
-        return carry
-
-    lax.fori_loop(0, 8, serve_upstream, 0)
-    normed_steps = rows_first(part_n, gn, *for_normed)
-    drive(value_steps)
-    drive(normed_steps)
-    drive(gate_steps)
     finish(state_steps)
-    drive(value_steps)
-    drive(normed_steps)
-    drive(gate_steps)
     drive(normed_steps)
     finish(value_steps)
     finish(gate_steps)
@@ -502,15 +671,16 @@
             jax.ShapeDtypeStruct((128, 512), F32),
             jax.ShapeDtypeStruct((128, 512), F32),
             jax.ShapeDtypeStruct((16, 8, 384), F32),
+            jax.ShapeDtypeStruct((128, 512), BF16),
         ),
         in_specs=[vmem()] * 8,
-        out_specs=(vmem(),) * 8,
+        out_specs=(vmem(),) * 9,
         scratch_shapes=[
             pltpu.VMEM((8, 128, 512), F32),
             pltpu.VMEM((8, 128, 512), F32),
             pltpu.VMEM((8, 128, 512), F32),
             sem((3,)), sem((3,)),
-        ] + [sem((8,))] * 4 + total_scratch() + gather_scratch() + across_scratch() + rows_scratch() * 2,
+        ] + [sem((2, 8))] * 4 + total_scratch() + gather_scratch(4) * 2 + across_scratch() + rows_scratch() * 2,
         compiler_params=params(0),
         cost_estimate=pl.CostEstimate(flops=3 * 10**9, bytes_accessed=200 * 10**6, transcendentals=0),
         name="project",
@@ -544,13 +714,10 @@
     return jnp.concatenate([jnp.where(lane < 64, pair, 0.0), jnp.where(lane < 64, 0.0, pair)], axis=0)
 
 
-def mix_kernel(
-    gate, value, gn, state, heads, gain,
-    normed, gate_low, value_low, backs, small,
+def mix_steps(
+    gate, value, gn, state, heads, gain, normed, gate_low, value_low, backs, small,
     step_rows, mixed, gated, d_mixed, part, slots, send, recv,
 ):
-    devices = [tensor_peer(j) for j in range(1, 16)]
-    announce(devices)
     me = tensor_place(0)
     b = state[:, :, 0:128].reshape(128, 128)
     c = state[:, :, 128:256].reshape(128, 128)
@@ -576,7 +743,7 @@
     square = jnp.sum(gated[...] * gated[...], axis=1, keepdims=True)
     inner = jnp.sum(gn[...] * gain[...] * gated[...], axis=1, keepdims=True)
     part[...] = jnp.where(lane == 0, square, jnp.where(lane == 1, inner, 0.0)).T[0:8, :]
-    gathered(len(devices))
+    yield
 
     def copy(j):
         return remote(part, slots.at[me], send.at[j], recv.at[j], tensor_peer(j))
@@ -584,6 +751,7 @@
     for j in range(1, 16):
         copy(j).start()
     slots[me] = part[...]
+    yield
     for j in range(1, 16):
         copy(j).wait()
     sums = slots[0]
@@ -597,6 +765,7 @@
     pull = token_cols[:, 1:2]
     unit = gated[...] * inv
     normed[...] = (unit * gain[...]).astype(BF16)
+    yield
     gain_sum = jnp.sum(gn[...] * unit, axis=0, keepdims=True)
     grad = inv * (gn[...] * gain[...]) - gated[...] * pull
     g = gate[...]
@@ -647,31 +816,22 @@
     small[8:16, 0:128] = jnp.where(lane8 == 0, bias_sum, jnp.where(lane8 == 1, decay_sum, 0.0))
 
 
-def mix(*args):
+def mix_scratch():
     sem = pltpu.SemaphoreType.DMA
-    return pl.pallas_call(
-        mix_kernel,
-        out_shape=(
-            jax.ShapeDtypeStruct((128, 512), BF16),
-            jax.ShapeDtypeStruct((128, 512), BF16),
-            jax.ShapeDtypeStruct((128, 512), BF16),
-            jax.ShapeDtypeStruct((128, 384), F32),
-            jax.ShapeDtypeStruct((16, 384), F32),
-        ),
-        in_specs=[vmem()] * 6,
-        out_specs=(vmem(),) * 5,
-        scratch_shapes=[
-            pltpu.VMEM((128, 128), F32),
-            pltpu.VMEM((128, 512), F32),
-            pltpu.VMEM((128, 512), F32),
-            pltpu.VMEM((128, 512), F32),
-            pltpu.VMEM((8, 128), F32),
-            pltpu.VMEM((16, 8, 128), F32),
-            sem((16,)), sem((16,)),
-        ],
-        compiler_params=params(1),
-        name="mix",
-    )(*args)
+    return [
+        pltpu.VMEM((128, 512), BF16),
+        pltpu.VMEM((128, 512), BF16),
+        pltpu.VMEM((128, 512), BF16),
+        pltpu.VMEM((128, 384), F32),
+        pltpu.VMEM((16, 384), F32),
+        pltpu.VMEM((128, 128), F32),
+        pltpu.VMEM((128, 512), F32),
+        pltpu.VMEM((128, 512), F32),
+        pltpu.VMEM((128, 512), F32),
+        pltpu.VMEM((8, 128), F32),
+        pltpu.VMEM((16, 8, 128), F32),
+        sem((16,)), sem((16,)),
+    ]
 
 
 def small_steps(grads, half, total, slots, own, full, c_send, c_recv, s_send, s_recv, g_send, g_recv, e_send, e_recv):
@@ -733,17 +893,21 @@
 
 
 def output_kernel(
-    normed, gate_low, value_low, backs, small, tok, tokc, upc, wcat, wof, s_in, s_out, s_step,
+    gate, value, gn, state, heads, gain, slab, s_in, s_out, s_step, tokc_far, upc_far, wcat_far, wof_far,
     layer_out, input_grad, grad_gate, grad_value, grad_output, grad_in, grad_out, grad_step, grad_small,
-    all_n, all_g, all_v, part_l, part_d, side, low, g_send, g_recv, grads, grads_in, h_send, h_recv, *scratch,
+    all_n, all_g, all_v, part_l, part_d, side, low, grads, grads_in, h_send, h_recv,
+    tokc, upc, wcat, wof, loaded, tok_t, up_t, *scratch,
 ):
     x_hi, y, core, x_lo, z = coords()
     chip = x_hi * 4 + y
+    for_mix, scratch = scratch[:13], scratch[13:]
+    normed, gate_low, value_low, backs, small = for_mix[:5]
     for_total, scratch = scratch[:8], scratch[8:]
     for_small, scratch = scratch[:14], scratch[14:]
     for_layer, scratch = scratch[:12], scratch[12:]
     for_input, scratch = scratch[:12], scratch[12:]
-    gather_layer, gather_input = scratch[:4], scratch[4:]
+    gather_layer, gather_input, scratch = scratch[:4], scratch[4:8], scratch[8:]
+    for_n, for_g, for_v = scratch[:4], scratch[4:8], scratch[8:]
     partner = core_peer()
     turned, turner, stays = turn_peers()
     devices = [chip_peer(j) for j in range(1, 8)] + [partner] + [tensor_peer(j) for j in range(1, 16)]
@@ -753,40 +917,90 @@
     def _():
         announce([turned, turner])
 
+    loads = [
+        pltpu.make_async_copy(source, target, loaded.at[i])
+        for i, (source, target) in enumerate(((tokc_far, tokc), (upc_far, upc), (wof_far, wof), (wcat_far, wcat)))
+    ]
+    for load in loads:
+        load.start()
+    mixing = mix_steps(gate, value, gn, state, heads, gain, *for_mix)
+    drive(mixing)
     gathered(len(devices) + jnp.where(stays, 0, 2))
-    sources = (normed, gate_low, value_low)
-    targets = (all_n, all_g, all_v)
-
-    def copy(i, j):
-        return remote(sources[i], targets[i].at[chip], g_send.at[i, j], g_recv.at[i, j], chip_peer(j))
-
-    for j in range(1, 8):
-        copy(0, j).start()
+    drive(mixing)
+
+    def turn_over(array, target):
+        def columns(index, carry):
+            at = pl.ds(pl.multiple_of(index * 256, 256), 256)
+            target[at, :] = array[:, :, at].reshape(1024, 256).T
+            return carry
+
+        lax.fori_loop(0, 4, columns, 0)
+
+    loads[0].wait()
+    turn_over(tokc, tok_t)
+    drive(mixing)
+    all_n[chip] = normed[...]
+
+    def chips_of(array):
+        return lambda at_side, level: array.at[at_side * 4 + level]
+
+    n_steps = gather_steps(along_y(), chips_of(all_n), *for_n)
+    g_steps = gather_steps(along_y(), chips_of(all_g), *for_g)
+    v_steps = gather_last_across(all_v, *for_v)
+    drive(n_steps)
+    finish(mixing)
+    all_g[chip] = gate_low[...]
+    all_v[chip] = value_low[...]
+    drive(g_steps)
+    drive(v_steps)
+    drive(n_steps)
     back_part, back_full = for_total[0], for_total[7]
     back_part[...] = backs[...].reshape(16, 8, 384)
     back_steps = total_steps(back_part, for_total[1], for_total[2], back_full, *for_total[3:7])
     drive(back_steps)
-    for i in range(3):
-        targets[i][chip] = sources[i][...]
-    for j in range(1, 8):
-        copy(0, j).wait_recv()
-    for i in (1, 2):
-        for j in range(1, 8):
-            copy(i, j).start()
-
-    def store(part, index, block):
-        row = 2 * ((y + 4 - index % 4) % 4)
-        part[row, index // 4] = block[:, :512]
-        part[row + 1, index // 4] = block[:, 512:]
-
-    def out_block(index, carry):
-        store(part_l, index, dot_cols(all_n[index], wof[...]))
+    drive(g_steps)
+    loads[1].wait()
+    turn_over(upc, up_t)
+    drive(v_steps)
+    drive(n_steps)
+    drive(g_steps)
+    drive(v_steps)
+    finish(n_steps)
+    loads[2].wait()
+    loads[3].wait()
+
+    def store(part, n, block):
+        for index in range(8):
+            row = 2 * ((y + 4 - index % 4) % 4) + n // 2
+            at = pl.ds(pl.multiple_of((n % 2) * 256, 256), 256)
+            part[row, index // 4, :, at] = block[128 * index : 128 * index + 128, :]
+
+    def weight_rows(n):
+        return pl.ds(pl.multiple_of(n * 256, 256), 256)
+
+    def out_block(n, carry):
+        store(part_l, n, dot_cols(all_n[...].reshape(1024, 512), wof[weight_rows(n), :]))
         return carry
 
-    lax.fori_loop(0, 8, out_block, 0)
+    lax.fori_loop(0, 4, out_block, 0)
     layer_steps = reduce_steps(part_l, *for_layer)
     drive(layer_steps)
     drive(back_steps)
+    finish(g_steps)
+    finish(v_steps)
+
+    def dense_block(n, carry):
+        store(
+            part_d, n,
+            dot_cols(all_g[...].reshape(1024, 512), wcat[weight_rows(n), 0:512])
+            + dot_cols(all_v[...].reshape(1024, 512), wcat[weight_rows(n), 512:1024]),
+        )
+        return carry
+
+    lax.fori_loop(0, 4, dense_block, 0)
+    input_steps = reduce_steps(part_d, *for_input)
+    drive(input_steps)
+    drive(layer_steps, 2)
 
     theirs = pl.ds(pl.multiple_of((1 - core) * 512, 512), 512)
     mine = pl.ds(pl.multiple_of(core * 512, 512), 512)
@@ -795,47 +1009,35 @@
         return remote(grads.at[i, theirs], grads_in.at[i], h_send.at[i], h_recv.at[i], partner)
 
     def weight_grad(i, left, right):
-        def rows(index, carry):
-            at = pl.ds(pl.multiple_of(index * 256, 256), 256)
-            grads[i, at, :] = dot_rows(left[:, :, at].reshape(1024, 256), right[...].reshape(1024, 512))
-            return carry
-
-        lax.fori_loop(0, 4, rows, 0)
+        def rows(half):
+            def block(index, carry):
+                at = pl.ds(pl.multiple_of(half * 512 + index * 256, 256), 256)
+                grads[i, at, :] = dot(left[at, :], right[...].reshape(1024, 512))
+                return carry
+
+            lax.fori_loop(0, 2, block, 0)
+
+        rows(1 - core)
         grad_copy(i).start()
-
-    drive(layer_steps)
-    weight_grad(0, upc, all_n)
-    drive(layer_steps)
+        rows(core)
+
     finish(back_steps)
     low[...] = back_full[...].reshape(128, 384).astype(BF16)
     side[...] = (
         dot_cols(low[:, 0:128], s_in[...]) + dot_cols(low[:, 128:256], s_out[...])
         + dot_cols(low[:, 256:384], s_step[...])
     )
-    slab = tok[:, pl.ds(pl.multiple_of((x_lo * 8 + z) * 512, 512), 512)]
     state_grads = jnp.concatenate(
-        [dot_rows(slab, low[...]), small[...], jnp.zeros((112, 384), F32)], axis=0
+        [dot_rows(slab[...], low[...]), small[...], jnp.zeros((112, 384), F32)], axis=0
     )
     for_small[0][...] = state_grads.reshape(2, 8, 40, 384)
     sum_steps = small_steps(*for_small)
     drive(sum_steps)
     drive(layer_steps)
-
-    for i in (1, 2):
-        for j in range(1, 8):
-            copy(i, j).wait_recv()
-
-    def dense_block(index, carry):
-        store(
-            part_d, index, dot_cols(all_g[index], wcat[:, 0:512]) + dot_cols(all_v[index], wcat[:, 512:1024])
-        )
-        return carry
-
-    lax.fori_loop(0, 8, dense_block, 0)
-    input_steps = reduce_steps(part_d, *for_input)
     drive(input_steps)
+    drive(sum_steps)
     drive(layer_steps)
-    drive(sum_steps)
+    weight_grad(0, up_t, all_n)
     drive(input_steps)
     drive(layer_steps)
     drive(sum_steps)
@@ -843,28 +1045,30 @@
     finish(layer_steps)
 
     def blocks_of(result):
-        def block(at_side, level):
-            return result.at[:, pl.ds(pl.multiple_of((at_side * 8 + level) * 512, 512), 512)]
+        def block(at_side, level, half):
+            columns = pl.ds(pl.multiple_of((at_side * 8 + level) * 512, 512), 512)
+            return result.at[:, columns] if half is None else result.at[pl.ds(64 * half, 64), columns]
 
         return block
 
     own = pl.ds(pl.multiple_of((x_lo * 8 + z) * 512, 512), 512)
     layer_out[:, own] = for_layer[9][...]
-    layer_gather = gather_steps(blocks_of(layer_out), *gather_layer)
-    drive(layer_gather)
-    weight_grad(1, tokc, all_g)
-    drive(input_steps)
-    drive(layer_gather)
-    drive(sum_steps)
-    drive(input_steps)
+    layer_gather = spread_steps(blocks_of(layer_out), *gather_layer)
     drive(layer_gather)
     drive(input_steps)
+    drive(sum_steps)
     drive(layer_gather)
-    weight_grad(2, tokc, all_v)
+    drive(input_steps)
+    weight_grad(1, tok_t, all_g)
+    drive(layer_gather)
     finish(input_steps)
     input_grad[:, own] = (for_input[9][...] + side[...]).astype(BF16)
-    input_gather = gather_steps(blocks_of(input_grad), *gather_input)
+    input_gather = spread_steps(blocks_of(input_grad), *gather_input)
     drive(input_gather)
+    drive(layer_gather)
+    weight_grad(2, tok_t, all_v)
+    drive(input_gather)
+    drive(layer_gather)
     finish(layer_gather)
     finish(sum_steps)
     summed = for_small[5][...].reshape(640, 384)
@@ -874,17 +1078,13 @@
     grad_small[...] = summed[512:528, :]
     drive(input_gather)
     outs = (grad_output, grad_gate, grad_value)
-    for i in range(2):
+    for i in range(3):
         grad_copy(i).wait_recv()
         outs[i][...] = grads[i, mine, :] + grads_in[i]
-    drive(input_gather)
-    grad_copy(2).wait_recv()
-    grad_value[...] = grads[2, mine, :] + grads_in[2]
+    drive(input_gather, 2)
     finish(input_gather)
     for i in range(3):
         grad_copy(i).wait_send()
-        for j in range(1, 8):
-            copy(i, j).wait_send()
 
 
 def outputs(*args):
@@ -902,7 +1102,7 @@
             jax.ShapeDtypeStruct((512, 128), F32),
             jax.ShapeDtypeStruct((16, 384), F32),
         ),
-        in_specs=[vmem()] * 13,
+        in_specs=[vmem()] * 10 + [pl.BlockSpec(memory_space=pl.ANY)] * 4,
         out_specs=(vmem(),) * 9,
         scratch_shapes=[
             pltpu.VMEM((8, 128, 512), BF16),
@@ -912,34 +1112,70 @@
             pltpu.VMEM((8, 2, 128, 512), F32),
             pltpu.VMEM((128, 512), F32),
             pltpu.VMEM((128, 384), BF16),
-            sem((3, 8)), sem((3, 8)),
             pltpu.VMEM((3, 1024, 512), F32),
             pltpu.VMEM((3, 512, 512), F32),
             sem((3,)), sem((3,)),
+            pltpu.VMEM((8, 128, 1024), BF16),
+            pltpu.VMEM((8, 128, 1024), BF16),
+            pltpu.VMEM((1024, 1024), BF16),
+            pltpu.VMEM((1024, 512), BF16),
+            sem((4,)),
+            pltpu.VMEM((1024, 1024), BF16),
+            pltpu.VMEM((1024, 1024), BF16),
         ]
-        + total_scratch() + [pltpu.VMEM((16, 8, 384), F32)]
-        + small_scratch() + reduce_scratch(BF16) + reduce_scratch(F32) + gather_scratch() * 2,
+        + mix_scratch() + total_scratch() + [pltpu.VMEM((16, 8, 384), F32)]
+        + small_scratch() + reduce_scratch(BF16) + reduce_scratch(F32) + spread_scratch() * 2
+        + gather_scratch(2) * 2 + last_across_scratch(),
         compiler_params=params(2),
         cost_estimate=pl.CostEstimate(flops=6 * 10**9, bytes_accessed=300 * 10**6, transcendentals=0),
         name="outputs",
     )(*args)
 
 
+def settle_kernel(*refs):
+    count = (len(refs) - 2) // 3
+    ins, outs, boxes = refs[:count], refs[count : 2 * count], refs[2 * count : 3 * count]
+    in_sems, out_sems = refs[-2:]
+    loads = [pltpu.make_async_copy(ins[i], boxes[i], in_sems.at[i]) for i in range(count)]
+    stores = [pltpu.make_async_copy(boxes[i], outs[i], out_sems.at[i]) for i in range(count)]
+    for load in loads:
+        load.start()
+    for load, store in zip(loads, stores):
+        load.wait()
+        store.start()
+    for store in stores:
+        store.wait()
+
+
+def settle(*arrays):
+    anywhere = pl.BlockSpec(memory_space=pl.ANY)
+    sem = pltpu.SemaphoreType.DMA
+    return pl.pallas_call(
+        settle_kernel,
+        out_shape=tuple(jax.ShapeDtypeStruct(a.shape, a.dtype) for a in arrays),
+        in_specs=[anywhere] * len(arrays),
+        out_specs=(anywhere,) * len(arrays),
+        scratch_shapes=[pltpu.VMEM(a.shape, a.dtype) for a in arrays] + [sem((len(arrays),)), sem((len(arrays),))],
+        compiler_params=pltpu.CompilerParams(vmem_limit_bytes=VMEM_LIMIT),
+        name="settle",
+    )(*arrays)
+
+
 def per_device(
     tokens_in, proj_gate, proj_value, state_in, state_out, proj_step,
     step_bias, decay_log, skip_scale, norm_gain, proj_output, upstream,
 ):
-    tokc, upc, wcat, wof, gate, value, gn, state = project(
+    tokc, upc, wcat, wof, gate, value, gn, state, slab = project(
         tokens_in, upstream, proj_gate, proj_value, proj_output, state_in, state_out, proj_step
     )
     heads = jnp.pad(jnp.stack([step_bias, decay_log, skip_scale], axis=1), ((0, 0), (0, 125)))
-    normed, gate_low, value_low, backs, small = mix(gate, value, gn, state, heads, norm_gain.reshape(1, 512))
+    *results, sums = outputs(
+        gate, value, gn, state, heads, norm_gain.reshape(1, 512), slab, state_in, state_out, proj_step,
+        tokc, upc, wcat, wof,
+    )
     (
-        layer_out, input_grad, grad_gate, grad_value, grad_output,
-        grad_state_in, grad_state_out, grad_step, sums,
-    ) = outputs(
-        normed, gate_low, value_low, backs, small, tokens_in, tokc, upc, wcat, wof, state_in, state_out, proj_step
-    )
+        layer_out, input_grad, grad_gate, grad_value, grad_output, grad_state_in, grad_state_out, grad_step,
+    ) = settle(*results)
     grad_gain = jnp.concatenate([sums[0], sums[1, :128]])
     grad_skip = jnp.concatenate([sums[2], sums[3, :128]]).reshape(8, 64).sum(axis=1)
     return (

time: 292 us -> 256 us (0.88)
  Pallas kernels: 272 us -> 251 us
  local copies, waits for them, and re-layouts: 16.2 us -> 2.99 us
    unnamed x22 -> x2, local copies, waits for them, and re-layouts: 10.9 us -> 0.01 us
    pallas_call x1, Pallas kernels: 111 us -> 102 us  [project(): pl.pallas_call(project_kernel, out_shape=(jax.ShapeDtypeStruct((8, 128, 1...]
    pallas_call x1, Pallas kernels: 12.5 us -> 6.05 us  [settle(): pl.pallas_call(settle_kernel, out_shape=tuple((jax.ShapeDtypeStruct(a.sha...]
    pallas_call x1, Pallas kernels: 149 us -> 143 us  [outputs(): pl.pallas_call(output_kernel, out_shape=(jax.ShapeDtypeStruct((128, 8192)...]
where the time goes in v2:
time: 256 us
  Pallas kernels  251 us (98%)
  local copies, waits for them, and re-layouts  2.99 us (1%)
    pallas_call x1, Pallas kernels, outputs(): pl.pallas_call(output_kernel, out_shape=(jax.ShapeDtypeStruct((128, 8192)...  143 us
    pallas_call x1, Pallas kernels, project(): pl.pallas_call(project_kernel, out_shape=(jax.ShapeDtypeStruct((8, 128, 1...  102 us
    pallas_call x1, Pallas kernels, settle(): pl.pallas_call(settle_kernel, out_shape=tuple((jax.ShapeDtypeStruct(a.sha...  6.05 us

profile of v2, /device:TPU:2, one launch (start us, length us, event | category | flops | bytes accessed | tf_op | source)
XLA Modules:
  0.0 256.2 jit_solution(15255169259297356838)
XLA Ops:
  0.6 0.7 copy.30
  1.4 0.7 copy.31
  2.1 0.7 copy.32
  2.8 0.7 select_maximum_fusion.heads
  3.5 101.7 %project.1 = (bf16[8,128,1024]{2,1,0:T(8,128)(2,1)}, bf16[8,128,1024]{2,1,0:T(8,128)(2,1)}, bf16[1024,1024]{1,0:T(8,128)(2,1)}, bf16[1024,512]{1,0:T(8,128)(2,1)...) custom-call(bf16[128,8192]{1,0:T(8,128)(2,1)} %tok.1, ...), custom_call_target="tpu_custom_call" | custom-call | flops 3000000000 | bytes 200000000 | tf_op jit(solution)/shard_map/project/pallas_call | solution.py:663
  105.2 142.9 %outputs.1 = (bf16[128,8192]{1,0:T(8,128)(2,1)}, bf16[128,8192]{1,0:T(8,128)(2,1)}, f32[512,512]{1,0:T(8,128)}, f32[512,512]{1,0:T(8,128)}, f32[512,512]{1,0:T(8...) custom-call(f32[128,512]{1,0:T(8,128)} %get-tuple-element.38.gate, ...), custom_call_target="tpu_custom_call" | custom-call | flops 6000000000 | bytes 300000000 | tf_op jit(solution)/shard_map/outputs/pallas_call | solution.py:1092
  248.1 0.0 copy-start
  248.1 6.1 %settle.1 = (bf16[128,8192]{1,0:T(8,128)(2,1)}, bf16[128,8192]{1,0:T(8,128)(2,1)}, f32[512,512]{1,0:T(8,128)}, f32[512,512]{1,0:T(8,128)}, f32[512,512]{1,0:T(8,...) custom-call(bf16[128,8192]{1,0:T(8,128)(2,1)} %get-tuple-element.47.refs_0_, ...), custom_call_target="tpu_custom_call" | custom-call | tf_op jit(solution)/shard_map/settle/pallas_call | solution.py:1153
  254.1 0.0 copy-done
  254.2 0.7 slice_reduce_fusion
  254.9 0.6 pad_maximum_fusion
  255.5 0.1 reshape.31
  255.5 0.6 reduce_sum.9
  (2 shorter events, 0.0 us)
Async XLA Ops:
  248.1 6.1 %copy-start = (f32[16,384]{1,0:T(8,128)S(1)}, f32[16,384]{1,0:T(8,128)}, u32[]{:S(2)}) copy-start(f32[16,384]{1,0:T(8,128)} %get-tuple-element.63) | copy-start | bytes 73732

commit v3 on v2

--- a/solution.py
+++ b/solution.py
@@ -12,6 +12,7 @@
 F32 = jnp.float32
 BF16 = jnp.bfloat16
 VMEM_LIMIT = 60 * 2**20
+ORDER = "DL1BDLSD2LDSlGDSGDGdHGHGgsHwHH"
 
 
 def coords():
@@ -197,48 +198,6 @@
     return [sem, sem, sem((2, count, 2)), sem((2, count, 2))]
 
 
-def gather_last_across(array, d_send, d_recv, x_send, x_recv):
-    x_hi, y, core, x_lo, z = coords()
-    ways = (place(x_hi, (y + 1) % 4, core, x_lo, z), place(x_hi, (y + 3) % 4, core, x_lo, z))
-    across = place(1 - x_hi, y, core, x_lo, z)
-
-    def near(way):
-        ref = array.at[x_hi * 4 + y]
-        return remote(ref, ref, d_send.at[way, 0], d_recv.at[way, 0], ways[way])
-
-    def far(way):
-        ref = array.at[x_hi * 4 + (y + 3 + 2 * way) % 4, pl.ds(64 * way, 64)]
-        return remote(ref, ref, d_send.at[way, 1], d_recv.at[way, 1], ways[way])
-
-    def cross(i):
-        ref = array.at[x_hi * 4 + (y + i) % 4]
-        return remote(ref, ref, x_send.at[i], x_recv.at[i], across)
-
-    for way in (0, 1):
-        near(way).start()
-    cross(0).start()
-    yield
-    for way in (0, 1):
-        near(way).wait_recv()
-        far(way).start()
-        cross(3 - 2 * way).start()
-    yield
-    for way in (0, 1):
-        far(way).wait_recv()
-    cross(2).start()
-    yield
-    for i in range(4):
-        cross(i).wait()
-    for way in (0, 1):
-        near(way).wait_send()
-        far(way).wait_send()
-
-
-def last_across_scratch():
-    sem = pltpu.SemaphoreType.DMA
-    return [sem((2, 2)), sem((2, 2)), sem((4,)), sem((4,))]
-
-
 def turn_peers():
     x_hi, y, core, x_lo, z = coords()
     turned = place(x_lo, (y + 4 - z // 2) % 4, core, x_hi, y * 2 + z % 2)
@@ -408,34 +367,42 @@
     return [sem((2, 6)), sem((2, 6)), sem((4,)), sem((4,))]
 
 
-def rows_first(part, result, inbox, send, recv, xin, x_send, x_recv):
+def rows_first(part, result, outbox, inbox, send, recv, xin, x_send, x_recv):
     x_hi, y, core, x_lo, z = coords()
     ways = (place(x_hi, (y + 1) % 4, core, x_lo, z), place(x_hi, (y + 3) % 4, core, x_lo, z))
     across = place(1 - x_hi, y, core, x_lo, z)
 
     def copy(way, step, block):
         level = (y + 2) % 4 if step == 0 else (y + 1 + 2 * way) % 4
+        source = part.at[block * 4 + level] if outbox is None else outbox.at[way, step, block]
         return remote(
-            part.at[block * 4 + level], inbox.at[way, step, block],
-            send.at[way, step, block], recv.at[way, step, block], ways[way],
+            source, inbox.at[way, step, block], send.at[way, step, block], recv.at[way, step, block], ways[way]
         )
 
-    for way in (0, 1):
-        copy(way, 0, way).start()
-    for way in (0, 1):
-        copy(way, 1, 1 - way).start()
+    def push(way, step, block):
+        level = (y + 2) % 4 if step == 0 else (y + 1 + 2 * way) % 4
+        if outbox is not None:
+            outbox[way, step, block] = part[block * 4 + level].astype(outbox.dtype)
+        copy(way, step, block).start()
+
+    for way in (0, 1):
+        push(way, 0, way)
+    for way in (0, 1):
+        push(way, 1, 1 - way)
     yield
     for way in (0, 1):
         copy(way, 0, way).wait_recv()
         level = (y + 1 + 2 * way) % 4
-        part[way * 4 + level] = part[way * 4 + level] + inbox[way, 0, way]
-        copy(way, 1, way).start()
+        part[way * 4 + level] = part[way * 4 + level] + inbox[way, 0, way].astype(F32)
+        push(way, 1, way)
     yield
     cross = remote(part.at[(1 - x_hi) * 4 + y], xin, x_send, x_recv, across)
     for block in (0, 1):
         for way in (0, 1):
             copy(way, 1, block).wait_recv()
-        part[block * 4 + y] = part[block * 4 + y] + (inbox[0, 1, block] + inbox[1, 1, block])
+        part[block * 4 + y] = part[block * 4 + y] + (
+            inbox[0, 1, block].astype(F32) + inbox[1, 1, block].astype(F32)
+        )
     cross.start()
     yield
     cross.wait()
@@ -446,14 +413,11 @@
             copy(way, 1, block).wait_send()
 
 
-def rows_scratch():
+def rows_scratch(kind):
     sem = pltpu.SemaphoreType.DMA
-    return [
-        pltpu.VMEM((2, 2, 2, 128, 512), F32),
-        sem((2, 2, 2)), sem((2, 2, 2)),
-        pltpu.VMEM((128, 512), F32),
-        sem, sem,
-    ]
+    out = pltpu.VMEM((2, 2, 2, 128, 512), kind)
+    boxes = [out] if kind == F32 else [out, out]
+    return boxes + [sem((2, 2, 2)), sem((2, 2, 2)), pltpu.VMEM((128, 512), F32), sem, sem]
 
 
 def across_first(part, result, xin, x_send, x_recv, inbox, send, recv):
@@ -522,8 +486,8 @@
 
 def project_kernel(
     tok, up, wg, wv, wo, s_in, s_out, s_step,
-    tokc, upc, wcat, wof, gate, value, gn, state, slab_out,
-    part_g, part_v, part_n, w_send, w_recv, p_send, p_recv, f_send, f_recv, *scratch,
+    tokc_far, upc_far, wcat_far, wof_far, slab_far, gate, value, gn, state,
+    tokc, upc, wcat, wof, slab_out, part_g, part_v, part_n, w_send, w_recv, p_send, p_recv, f_send, f_recv, *scratch,
 ):
     x_hi, y, core, x_lo, z = coords()
     chip = x_hi * 4 + y
@@ -531,7 +495,8 @@
     for_tokens, scratch = scratch[:4], scratch[4:]
     for_upstream, scratch = scratch[:4], scratch[4:]
     for_gate, scratch = scratch[:6], scratch[6:]
-    for_value, for_normed = scratch[:6], scratch[6:]
+    for_value, scratch = scratch[:6], scratch[6:]
+    for_normed, stored = scratch[:7], scratch[7]
 
     def to_chip(j):
         return ((x_hi + j // 4) % 2) * 4 + (y + j % 4) % 4
@@ -628,8 +593,14 @@
         lax.fori_loop(0, 2, columns, 0)
 
     gate_steps = across_first(part_g, gate, *for_gate)
-    value_steps = rows_first(part_v, value, *for_value)
+    value_steps = rows_first(part_v, value, None, *for_value)
     normed_steps = rows_first(part_n, gn, *for_normed)
+    stores = [
+        pltpu.make_async_copy(source, target, stored.at[i])
+        for i, (source, target) in enumerate(
+            ((tokc, tokc_far), (wcat, wcat_far), (wof, wof_far), (slab_out, slab_far), (upc, upc_far))
+        )
+    ]
     multiply(part_g, tokc, wcat, 0)
     drive(gate_steps)
     multiply(part_v, tokc, wcat, 512)
@@ -645,6 +616,8 @@
         full_copy(1, j).wait()
     multiply(part_n, upc, wof, 0)
     drive(normed_steps)
+    for store in stores:
+        store.start()
     drive(gate_steps)
     drive(state_steps)
     drive(normed_steps)
@@ -656,6 +629,8 @@
     finish(value_steps)
     finish(gate_steps)
     finish(normed_steps)
+    for store in stores:
+        store.wait()
 
 
 def project(*args):
@@ -667,20 +642,25 @@
             jax.ShapeDtypeStruct((8, 128, 1024), BF16),
             jax.ShapeDtypeStruct((1024, 1024), BF16),
             jax.ShapeDtypeStruct((1024, 512), BF16),
+            jax.ShapeDtypeStruct((128, 512), BF16),
             jax.ShapeDtypeStruct((128, 512), F32),
             jax.ShapeDtypeStruct((128, 512), F32),
             jax.ShapeDtypeStruct((128, 512), F32),
             jax.ShapeDtypeStruct((16, 8, 384), F32),
-            jax.ShapeDtypeStruct((128, 512), BF16),
         ),
         in_specs=[vmem()] * 8,
-        out_specs=(vmem(),) * 9,
+        out_specs=(pl.BlockSpec(memory_space=pl.ANY),) * 5 + (vmem(),) * 4,
         scratch_shapes=[
+            pltpu.VMEM((8, 128, 1024), BF16),
+            pltpu.VMEM((8, 128, 1024), BF16),
+            pltpu.VMEM((1024, 1024), BF16),
+            pltpu.VMEM((1024, 512), BF16),
+            pltpu.VMEM((128, 512), BF16),
             pltpu.VMEM((8, 128, 512), F32),
             pltpu.VMEM((8, 128, 512), F32),
             pltpu.VMEM((8, 128, 512), F32),
             sem((3,)), sem((3,)),
-        ] + [sem((2, 8))] * 4 + total_scratch() + gather_scratch(4) * 2 + across_scratch() + rows_scratch() * 2,
+        ] + [sem((2, 8))] * 4 + total_scratch() + gather_scratch(4) * 2 + across_scratch() + rows_scratch(F32) + rows_scratch(BF16) + [sem((5,))],
         compiler_params=params(0),
         cost_estimate=pl.CostEstimate(flops=3 * 10**9, bytes_accessed=200 * 10**6, transcendentals=0),
         name="project",
@@ -946,28 +926,22 @@
 
     n_steps = gather_steps(along_y(), chips_of(all_n), *for_n)
     g_steps = gather_steps(along_y(), chips_of(all_g), *for_g)
-    v_steps = gather_last_across(all_v, *for_v)
+    v_steps = gather_steps(along_y(), chips_of(all_v), *for_v)
     drive(n_steps)
     finish(mixing)
     all_g[chip] = gate_low[...]
     all_v[chip] = value_low[...]
+    drive(n_steps, 2)
     drive(g_steps)
     drive(v_steps)
-    drive(n_steps)
     back_part, back_full = for_total[0], for_total[7]
     back_part[...] = backs[...].reshape(16, 8, 384)
     back_steps = total_steps(back_part, for_total[1], for_total[2], back_full, *for_total[3:7])
     drive(back_steps)
-    drive(g_steps)
     loads[1].wait()
     turn_over(upc, up_t)
-    drive(v_steps)
-    drive(n_steps)
-    drive(g_steps)
-    drive(v_steps)
     finish(n_steps)
     loads[2].wait()
-    loads[3].wait()
 
     def store(part, n, block):
         for index in range(8):
@@ -983,11 +957,38 @@
         return carry
 
     lax.fori_loop(0, 4, out_block, 0)
+    theirs = pl.ds(pl.multiple_of((1 - core) * 512, 512), 512)
+    mine = pl.ds(pl.multiple_of(core * 512, 512), 512)
+
+    def grad_copy(i):
+        return remote(grads.at[i, theirs], grads_in.at[i], h_send.at[i], h_recv.at[i], partner)
+
+    def weight_grad(i, left, right):
+        def rows(half):
+            def block(index, carry):
+                at = pl.ds(pl.multiple_of(half * 512 + index * 256, 256), 256)
+                grads[i, at, :] = dot(left[at, :], right[...].reshape(1024, 512))
+                return carry
+
+            lax.fori_loop(0, 2, block, 0)
+
+        rows(1 - core)
+        grad_copy(i).start()
+        rows(core)
+
     layer_steps = reduce_steps(part_l, *for_layer)
     drive(layer_steps)
+    weight_grad(0, up_t, all_n)
+    drive(g_steps)
+    drive(v_steps)
+    drive(layer_steps)
+    drive(g_steps)
+    drive(v_steps)
     drive(back_steps)
+    drive(layer_steps)
     finish(g_steps)
     finish(v_steps)
+    loads[3].wait()
 
     def dense_block(n, carry):
         store(
@@ -999,50 +1000,20 @@
 
     lax.fori_loop(0, 4, dense_block, 0)
     input_steps = reduce_steps(part_d, *for_input)
-    drive(input_steps)
-    drive(layer_steps, 2)
-
-    theirs = pl.ds(pl.multiple_of((1 - core) * 512, 512), 512)
-    mine = pl.ds(pl.multiple_of(core * 512, 512), 512)
-
-    def grad_copy(i):
-        return remote(grads.at[i, theirs], grads_in.at[i], h_send.at[i], h_recv.at[i], partner)
-
-    def weight_grad(i, left, right):
-        def rows(half):
-            def block(index, carry):
-                at = pl.ds(pl.multiple_of(half * 512 + index * 256, 256), 256)
-                grads[i, at, :] = dot(left[at, :], right[...].reshape(1024, 512))
-                return carry
-
-            lax.fori_loop(0, 2, block, 0)
-
-        rows(1 - core)
-        grad_copy(i).start()
-        rows(core)
-
-    finish(back_steps)
-    low[...] = back_full[...].reshape(128, 384).astype(BF16)
-    side[...] = (
-        dot_cols(low[:, 0:128], s_in[...]) + dot_cols(low[:, 128:256], s_out[...])
-        + dot_cols(low[:, 256:384], s_step[...])
-    )
-    state_grads = jnp.concatenate(
-        [dot_rows(slab[...], low[...]), small[...], jnp.zeros((112, 384), F32)], axis=0
-    )
-    for_small[0][...] = state_grads.reshape(2, 8, 40, 384)
     sum_steps = small_steps(*for_small)
-    drive(sum_steps)
-    drive(layer_steps)
-    drive(input_steps)
-    drive(sum_steps)
-    drive(layer_steps)
-    weight_grad(0, up_t, all_n)
-    drive(input_steps)
-    drive(layer_steps)
-    drive(sum_steps)
-    drive(input_steps)
-    finish(layer_steps)
+
+    def state_products():
+        finish(back_steps)
+        low[...] = back_full[...].reshape(128, 384).astype(BF16)
+        side[...] = (
+            dot_cols(low[:, 0:128], s_in[...]) + dot_cols(low[:, 128:256], s_out[...])
+            + dot_cols(low[:, 256:384], s_step[...])
+        )
+        state_grads = jnp.concatenate(
+            [dot_rows(slab[...], low[...]), small[...], jnp.zeros((112, 384), F32)], axis=0
+        )
+        for_small[0][...] = state_grads.reshape(2, 8, 40, 384)
+        drive(sum_steps)
 
     def blocks_of(result):
         def block(at_side, level, half):
@@ -1052,36 +1023,49 @@
         return block
 
     own = pl.ds(pl.multiple_of((x_lo * 8 + z) * 512, 512), 512)
-    layer_out[:, own] = for_layer[9][...]
     layer_gather = spread_steps(blocks_of(layer_out), *gather_layer)
-    drive(layer_gather)
-    drive(input_steps)
-    drive(sum_steps)
-    drive(layer_gather)
-    drive(input_steps)
-    weight_grad(1, tok_t, all_g)
-    drive(layer_gather)
-    finish(input_steps)
-    input_grad[:, own] = (for_input[9][...] + side[...]).astype(BF16)
     input_gather = spread_steps(blocks_of(input_grad), *gather_input)
-    drive(input_gather)
-    drive(layer_gather)
-    weight_grad(2, tok_t, all_v)
-    drive(input_gather)
-    drive(layer_gather)
-    finish(layer_gather)
-    finish(sum_steps)
-    summed = for_small[5][...].reshape(640, 384)
-    grad_in[...] = summed[0:512, 0:128]
-    grad_out[...] = summed[0:512, 128:256]
-    grad_step[...] = summed[0:512, 256:384]
-    grad_small[...] = summed[512:528, :]
-    drive(input_gather)
+
+    def layer_turned():
+        finish(layer_steps)
+        layer_out[:, own] = for_layer[9][...]
+
+    def input_turned():
+        finish(input_steps)
+        input_grad[:, own] = (for_input[9][...] + side[...]).astype(BF16)
+
+    def state_results():
+        finish(sum_steps)
+        summed = for_small[5][...].reshape(640, 384)
+        grad_in[...] = summed[0:512, 0:128]
+        grad_out[...] = summed[0:512, 128:256]
+        grad_step[...] = summed[0:512, 256:384]
+        grad_small[...] = summed[512:528, :]
+
     outs = (grad_output, grad_gate, grad_value)
-    for i in range(3):
-        grad_copy(i).wait_recv()
-        outs[i][...] = grads[i, mine, :] + grads_in[i]
-    drive(input_gather, 2)
+
+    def weight_results():
+        for i in range(3):
+            grad_copy(i).wait_recv()
+            outs[i][...] = grads[i, mine, :] + grads_in[i]
+
+    actions = {
+        "D": lambda: drive(input_steps),
+        "d": input_turned,
+        "H": lambda: drive(input_gather),
+        "L": lambda: drive(layer_steps),
+        "l": layer_turned,
+        "G": lambda: drive(layer_gather),
+        "g": lambda: finish(layer_gather),
+        "B": state_products,
+        "S": lambda: drive(sum_steps),
+        "s": state_results,
+        "1": lambda: weight_grad(1, tok_t, all_g),
+        "2": lambda: weight_grad(2, tok_t, all_v),
+        "w": weight_results,
+    }
+    for action in ORDER:
+        actions[action]()
     finish(input_gather)
     for i in range(3):
         grad_copy(i).wait_send()
@@ -1125,7 +1109,7 @@
         ]
         + mix_scratch() + total_scratch() + [pltpu.VMEM((16, 8, 384), F32)]
         + small_scratch() + reduce_scratch(BF16) + reduce_scratch(F32) + spread_scratch() * 2
-        + gather_scratch(2) * 2 + last_across_scratch(),
+        + gather_scratch(2) * 3,
         compiler_params=params(2),
         cost_estimate=pl.CostEstimate(flops=6 * 10**9, bytes_accessed=300 * 10**6, transcendentals=0),
         name="outputs",
@@ -1165,7 +1149,7 @@
     tokens_in, proj_gate, proj_value, state_in, state_out, proj_step,
     step_bias, decay_log, skip_scale, norm_gain, proj_output, upstream,
 ):
-    tokc, upc, wcat, wof, gate, value, gn, state, slab = project(
+    tokc, upc, wcat, wof, slab, gate, value, gn, state = project(
         tokens_in, upstream, proj_gate, proj_value, proj_output, state_in, state_out, proj_step
     )
     heads = jnp.pad(jnp.stack([step_bias, decay_log, skip_scale], axis=1), ((0, 0), (0, 125)))

time: 256 us -> 249 us (0.973)
  Pallas kernels: 251 us -> 244 us
    pallas_call x1, Pallas kernels: 102 us -> 91.4 us  [project(): pl.pallas_call(project_kernel, out_shape=(jax.ShapeDtypeStruct((8, 128, 1...]
    pallas_call x1, Pallas kernels: 143 us -> 146 us  [outputs(): pl.pallas_call(output_kernel, out_shape=(jax.ShapeDtypeStruct((128, 8192)...]
where the time goes in v3:
time: 249 us
  Pallas kernels  244 us (98%)
  local copies, waits for them, and re-layouts  2.99 us (1%)
    pallas_call x1, Pallas kernels, outputs(): pl.pallas_call(output_kernel, out_shape=(jax.ShapeDtypeStruct((128, 8192)...  146 us
    pallas_call x1, Pallas kernels, project(): pl.pallas_call(project_kernel, out_shape=(jax.ShapeDtypeStruct((8, 128, 1...  91.4 us
    pallas_call x1, Pallas kernels, settle(): pl.pallas_call(settle_kernel, out_shape=tuple((jax.ShapeDtypeStruct(a.sha...  6.05 us

profile of v3, /device:TPU:2, one launch (start us, length us, event | category | flops | bytes accessed | tf_op | source)
XLA Modules:
  0.0 249.2 jit_solution(14884651988771056878)
XLA Ops:
  0.6 0.7 copy.30
  1.4 0.7 copy.31
  2.1 0.7 copy.32
  2.8 0.7 select_maximum_fusion.heads
  3.5 91.4 %project.1 = (bf16[8,128,1024]{2,1,0:T(8,128)(2,1)}, bf16[8,128,1024]{2,1,0:T(8,128)(2,1)}, bf16[1024,1024]{1,0:T(8,128)(2,1)}, bf16[1024,512]{1,0:T(8,128)(2,1)...) custom-call(bf16[128,8192]{1,0:T(8,128)(2,1)} %tok.1, ...), custom_call_target="tpu_custom_call" | custom-call | flops 3000000000 | bytes 200000000 | tf_op jit(solution)/shard_map/project/pallas_call | solution.py:638
  94.9 146.2 %outputs.1 = (bf16[128,8192]{1,0:T(8,128)(2,1)}, bf16[128,8192]{1,0:T(8,128)(2,1)}, f32[512,512]{1,0:T(8,128)}, f32[512,512]{1,0:T(8,128)}, f32[512,512]{1,0:T(8...) custom-call(f32[128,512]{1,0:T(8,128)} %get-tuple-element.38.gate, ...), custom_call_target="tpu_custom_call" | custom-call | flops 6000000000 | bytes 300000000 | tf_op jit(solution)/shard_map/outputs/pallas_call | solution.py:1076
  241.1 0.0 copy-start
  241.1 6.1 %settle.1 = (bf16[128,8192]{1,0:T(8,128)(2,1)}, bf16[128,8192]{1,0:T(8,128)(2,1)}, f32[512,512]{1,0:T(8,128)}, f32[512,512]{1,0:T(8,128)}, f32[512,512]{1,0:T(8,...) custom-call(bf16[128,8192]{1,0:T(8,128)(2,1)} %get-tuple-element.47.refs_0_, ...), custom_call_target="tpu_custom_call" | custom-call | tf_op jit(solution)/shard_map/settle/pallas_call | solution.py:1137
  247.1 0.0 copy-done
  247.2 0.7 slice_reduce_fusion
  247.9 0.6 pad_maximum_fusion
  248.5 0.1 reshape.31
  248.6 0.6 reduce_sum.9
  (2 shorter events, 0.0 us)
Async XLA Ops:
  241.1 6.1 %copy-start = (f32[16,384]{1,0:T(8,128)S(1)}, f32[16,384]{1,0:T(8,128)}, u32[]{:S(2)}) copy-start(f32[16,384]{1,0:T(8,128)} %get-tuple-element.63) | copy-start | bytes 73732
